TPU v7x, 256 devices: a whole 4x4x8 slice. The times are simulated.
256 devices in a mesh: amp: 32 (over y, x, core), int: 8 (over z).
Axes of the slice: x: 4, y: 4, z: 8, core: 2. Of those that a mesh axis runs over, the one named last changes fastest.
Arguments:
- amplitudes: float32 [1536, 1024], P('int'), may hold values from -6 to 6
- slab_integrals: float32 [1024, 51200], P('int', 'amp'), may hold values from -0.1875 to 0.1875
- cycle_integrals: float32 [96, 800, 1024], P('int', 'amp'), may hold values from -0.0390625 to 0.0390625
- occ_irrep: int32 [96], replicated, may hold values from 0 to 7
- vir_irrep: int32 [800], replicated, may hold values from 0 to 7
Outputs:
- ladder: float32 [1536, 51200], P('int', 'amp')
- cycle: float32 [1024, 1024], P('int', 'amp')
All inputs are finite; a program needn't handle non-finite values.
Results may differ from a plain program's by a relative error of at most 0.00011.
Values sent between devices are 32-bit elements; how exact they have to be, the bound alone decides.
A program may use at most 64 MiB of HBM per device.

v0:
```python
import jax
import jax.numpy as jnp
from jax import lax
from jax.sharding import PartitionSpec as P

NOCC = 96
NVIR = 800
SLAB = 64


def per_device(amplitudes, slab_integrals, cycle_integrals, occ_irrep, vir_irrep):
    rows = amplitudes.shape[0]
    width = slab_integrals.shape[1]
    ladder = jnp.dot(
        amplitudes,
        lax.all_gather(slab_integrals, "int", axis=0, tiled=True),
        precision=lax.Precision.HIGHEST,
        preferred_element_type=jnp.float32,
    )
    i_local = rows // NOCC
    a_local = width // NVIR
    blocks = ladder.reshape(i_local, NOCC, a_local, NVIR)
    columns = cycle_integrals.shape[2]
    moved = lax.all_to_all(
        lax.all_to_all(blocks, "amp", split_axis=3, concat_axis=2, tiled=True),
        "int",
        split_axis=1,
        concat_axis=0,
        tiled=True,
    )
    partial_value = jnp.einsum(
        "ikac,kcn->ian", moved, cycle_integrals, precision=lax.Precision.HIGHEST
    )
    partial_value = partial_value.reshape(moved.shape[0] * SLAB, columns)
    narrowed = lax.psum_scatter(partial_value, "amp", scatter_dimension=1, tiled=True)
    sums = lax.psum_scatter(narrowed, "int", scatter_dimension=0, tiled=True)
    col_local = sums.shape[1]
    row_start = lax.axis_index("int") * i_local
    batch_labels = lax.dynamic_slice_in_dim(occ_irrep, row_start, i_local, 0)
    slab_labels = vir_irrep[:SLAB]
    row_labels = jnp.bitwise_xor(batch_labels[:, None], slab_labels[None, :]).reshape(-1)
    col_ids = lax.axis_index("amp") * col_local + jnp.arange(col_local, dtype=jnp.int32)
    col_occ = col_ids // SLAB
    col_vir = col_ids % SLAB
    occ_match = col_occ[:, None] == jnp.arange(NOCC, dtype=jnp.int32)[None, :]
    vir_match = col_vir[:, None] == jnp.arange(SLAB, dtype=jnp.int32)[None, :]
    occ_lookup = jnp.sum(jnp.where(occ_match, occ_irrep[None, :], 0), axis=1)
    vir_lookup = jnp.sum(jnp.where(vir_match, slab_labels[None, :], 0), axis=1)
    col_labels = jnp.bitwise_xor(occ_lookup, vir_lookup)
    keep = row_labels[:, None] == col_labels[None, :]
    cycle = jnp.where(keep, sums, jnp.zeros_like(sums))
    return (ladder, cycle)


def solution(mesh):
    in_specs = (P("int", None), P("int", "amp"), P("int", "amp", None), P(), P())
    out_specs = (P("int", "amp"), P("int", "amp"))
    return jax.shard_map(
        per_device, mesh=mesh, in_specs=in_specs, out_specs=out_specs, check_vma=False
    )
```

profile of v0, /device:TPU:1, one launch (start us, length us, event | category | flops | bytes accessed | tf_op | source)
XLA Modules:
  0.0 336.9 jit_solution(13221892820689987820)
XLA Ops:
  7.2 0.0 copy-start
  7.2 0.0 all-gather.2.cloned.1.call-start
  7.2 0.7 all-gather.2.cloned.1.call-update
  7.9 0.0 reduce-scatter.3.cloned.1.call-start
  8.0 86.1 %all-gather.2.cloned.1.call-done = f32[1024,1600]{0,1:T(8,128)} async-done(((f32[128,1600]{0,1:T(8,128)}), f32[1024,1600]{0,1:T(8,128)}) %all-gather.2.cloned.1.call-update) | async-done | bytes 6553616 | tf_op jit(solution)/shard_map/all_gather | solution.py:16
  94.0 10.0 %fusion = f32[192,1600]{1,0:T(8,128)S(1)} fusion(f32[192,1024]{1,0:T(8,128)} %param.5, f32[1024,1600]{0,1:T(8,128)} %all-gather.2.cloned.1.call-done), kind=kOutput, calls=%fused_computation.13 | convolution fusion | flops 3774873600 | bytes 8568832 | tf_op jit(solution)/shard_map/dot_general | solution.py:14
  104.1 0.0 copy-start.1
  104.1 1.0 copy-done.1
  105.1 2.1 reshape.63
  107.2 4.3 %copy.25 = f32[2,96,2,800]{1,2,0,3:T(2,128)S(1)} copy(f32[2,96,2,800]{3,2,1,0:T(2,128)} %reshape.63) | data formatting | bytes 2457600 | tf_op jit(solution)/shard_map/reshape | solution.py:22
  111.5 34.0 %all_to_all.36 = f32[2,96,2,800]{1,2,0,3:T(2,128)S(1)} all-to-all(f32[2,96,2,800]{1,2,0,3:T(2,128)S(1)} %copy.25), channel_id=1, replica_groups=mesh['amp'=32,'int'=8] {'amp'}, dimensions={3} | all-to-all | bytes 2457600 | tf_op jit(solution)/shard_map/all_to_all | solution.py:25
  145.5 0.9 copy.27
  146.5 3.2 copy.28
  149.7 3.8 %reshape.65 = f32[8,1,38400]{2,1,0:T(1,128)S(1)} reshape(f32[96,25,2,64]{3,2,1,0:T(2,128)} %bitcast.22) | data formatting | bytes 2457600
  153.6 35.3 %all_to_all.37 = f32[8,1,38400]{2,1,0:T(1,128)} all-to-all(f32[8,1,38400]{2,1,0:T(1,128)S(1)} %reshape.65), channel_id=1, replica_groups=mesh['amp'=32,'int'=8] {'int'}, dimensions={0} | all-to-all | bytes 2457600 | tf_op jit(solution)/shard_map/all_to_all | solution.py:24
  188.9 0.5 broadcast.82
  189.4 4.9 %reduce = f32[8,38400]{1,0:T(8,128)S(1)} reduce(f32[8,1,38400]{2,1,0:T(1,128)} %all_to_all.37, f32[]{:T(128)} %broadcast.82), dimensions={1}, to_apply=%all_to_all.30.reduce_sub_computation | reduce | bytes 2457604 | tf_op jit(solution)/shard_map/all_to_all | solution.py:24
  194.2 3.2 reshape.66
  197.4 4.0 %copy.29 = f32[8,2,12,64,25]{3,1,0,4,2:T(2,128)} copy(f32[8,2,12,64,25]{3,1,4,2,0:T(2,128)} %bitcast.23) | data formatting | bytes 2457600 | tf_op jit(solution)/shard_map/all_to_all | solution.py:24
  201.4 2.2 dot_general.12
  203.6 0.0 copy-done
  203.6 8.3 %convolution_bitcast_fusion = f32[1024,1024]{0,1:T(8,128)} fusion(f32[1024,25,12]{0,1,2:T(8,128)S(1)} %dot_general.12, f32[12,25,1024]{2,1,0:T(8,128)S(1)} %copy-done), kind=kOutput, calls=%fused_computation | convolution fusion | flops 3774873600 | bytes 6651904 | tf_op jit(solution)/shard_map/ikac,kcn->ian/dot_general | solution.py:31
  211.9 0.0 copy-start.2
  211.9 0.0 reduce-scatter.3.cloned.1.call-update
  211.9 0.0 reduce-scatter.5.cloned.1.call-start
  212.0 0.7 slice.3
  212.7 0.0 copy-done.2
  212.7 0.1 dynamic_slice.3
  212.8 0.1 broadcast_xor_fusion
  212.8 81.4 %reduce-scatter.3.cloned.1.call-done = f32[1024,32]{0,1:T(8,128)} async-done(((f32[1024,1024]{0,1:T(8,128)}), f32[1024,32]{0,1:T(8,128)}) %reduce-scatter.3.cloned.1.call-update) | async-done | bytes 131088 | tf_op jit(solution)/shard_map/reduce_scatter | solution.py:35
  294.2 0.0 reduce-scatter.5.cloned.1.call-update
  294.3 0.1 xor.30
  294.4 0.2 select_reduce_fusion.1
  294.5 0.2 select_reduce_fusion
  294.7 34.3 %reduce-scatter.5.cloned.1.call-done = f32[128,32]{0,1:T(8,128)} async-done(((f32[1024,32]{0,1:T(8,128)}), f32[128,32]{0,1:T(8,128)}) %reduce-scatter.5.cloned.1.call-update) | async-done | bytes 16400 | tf_op jit(solution)/shard_map/reduce_scatter | solution.py:36
  329.0 1.4 compare_select_fusion
  (2 shorter events, 0.0 us)
Async XLA Ops:
  7.2 196.4 %copy-start = (f32[12,25,1024]{2,1,0:T(8,128)S(1)}, f32[12,25,1024]{2,1,0:T(8,128)}, u32[]{:S(2)}) copy-start(f32[12,25,1024]{2,1,0:T(8,128)} %param.7) | copy-start | bytes 3686404
  7.2 86.9 %all-gather.2.cloned.1.call-start = ((), (), s32[]{:S(2)}) async-start(), calls=%async_computation.4 | async-start | bytes 7372800 | tf_op jit(solution)/shard_map/all_gather | solution.py:16
  7.9 286.3 %reduce-scatter.3.cloned.1.call-start = ((), (), s32[]{:S(2)}) async-start(), calls=%async_computation.5 | async-start | bytes 4325376 | tf_op jit(solution)/shard_map/reduce_scatter | solution.py:35
  104.1 1.0 copy-start.1
  211.9 0.8 copy-start.2
  211.9 117.1 %reduce-scatter.5.cloned.1.call-start = ((), (), s32[]{:S(2)}) async-start(), calls=%async_computation.6 | async-start | bytes 147456 | tf_op jit(solution)/shard_map/reduce_scatter | solution.py:36
Sparse Core Ops, SparseCore 0:
  9.7 84.2 all-gather.1
  212.1 82.1 reduce-scatter.2
  296.9 32.0 reduce-scatter.4
where the time goes:
time: 342 us; the launch traced here: 337 us
  waiting for transfers between devices  202 us (59%)
  blocking collectives  69.3 us (20%)
  local copies, waits for them, and re-layouts  26.2 us (8%)
  matrix products  18.3 us (5%)
  between operations  13.8 us (4%)
  other arithmetic  6.69 us (2%)
    all_gather x1, waiting for transfers between devices, per_device(): lax.all_gather(slab_integrals, 'int', axis=0, tiled=True)  86.1 us
    reduce_scatter x1, waiting for transfers between devices, per_device(): lax.psum_scatter(partial_value, 'amp', scatter_dimension=1, tiled=True)  81.4 us
    all_to_all x1, blocking collectives, per_device(): lax.all_to_all(lax.all_to_all(blocks, 'amp', split_axis=3, concat_axis=2,...  35.3 us
    reduce_scatter x1, waiting for transfers between devices, per_device(): sums = lax.psum_scatter(narrowed, 'int', scatter_dimension=0, tiled=True)  34.3 us
    all_to_all x1, blocking collectives, per_device(): lax.all_to_all(blocks, 'amp', split_axis=3, concat_axis=2, tiled=True)  34 us
    dot_general x1, matrix products, per_device(): jnp.dot(amplitudes, lax.all_gather(slab_integrals, 'int', axis=0, tiled=T...  10 us
    dot_general x1, matrix products, per_device(): jnp.einsum('ikac,kcn->ian', moved, cycle_integrals, precision=lax.Precisi...  8.31 us
    unnamed x8, local copies, waits for them, and re-layouts  8.11 us
  transfers between devices with their start and end apart: 3, of which 3 were waited for; matrix products, arithmetic and copies ran while one was open for 0% of the time, Pallas kernels for 0%

commit v1 on v0

v1 whole, which is shorter than its diff:
```python
import jax
import jax.numpy as jnp
from jax import lax
from jax.experimental import pallas as pl
from jax.experimental.pallas import tpu as pltpu
from jax.sharding import PartitionSpec as P

NOCC = 96
NVIR = 800
SLAB = 64
F32 = jnp.float32
BF16 = jnp.bfloat16
MESH = pl.DeviceIdType.MESH

AMP = 32
INT = 8
W0 = 896
W1 = 704
CUT1 = 768
WIDTHS = (W0, W1)
STARTS = (0, W0)
RIGHT, LEFT = 0, 1


def iota(shape, dim):
    return lax.broadcasted_iota(jnp.int32, shape, dim)


def split(x):
    high = x.astype(BF16)
    return high, (x - high.astype(F32)).astype(BF16)


def mm(a, b):
    return jnp.dot(a, b, preferred_element_type=F32)


def mm_nt(a, b):
    return lax.dot_general(a, b, (((1,), (1,)), ((), ())), preferred_element_type=F32)


def one_hot(match):
    return jnp.where(match, 1.0, 0.0).astype(BF16)


def body(
    amp_ref, slab_ref, w_ref,
    lad_ref, sum_ref,
    g0, g1, a3, l2, l2h, l2l, p0, p1, s_buf, t_buf, u_buf, v_buf,
    wpad, wx, whi, wlo, msg, rcv, ct, rs, sxy, zs, zr,
    ag_send, ag_recv, s_sem, u_sem, w_sem, a_send, a_recv, r_send, r_recv, z_sem,
):
    d = lax.axis_index("amp")
    z = lax.axis_index("int")
    core = lax.rem(d, 2)
    chip = d // 2
    row = d // 8
    tile = lax.rem(d, 8)
    sibling = d + 1 - 2 * core
    gather = (g0, g1)
    spread = (p0, p1)

    def around(step):
        return lax.rem(z + step + INT, INT)

    barrier = pltpu.get_barrier_semaphore()

    @pl.loop(1, AMP)
    def _(j):
        pl.semaphore_signal(barrier, inc=1, device_id={"amp": lax.rem(d + j, AMP), "int": z}, device_id_type=MESH)

    @pl.loop(1, INT)
    def _(j):
        up = lax.rem(z + j, INT)
        pl.semaphore_signal(barrier, inc=1, device_id={"amp": d, "int": up}, device_id_type=MESH)
        pl.semaphore_signal(barrier, inc=1, device_id={"amp": sibling, "int": up}, device_id_type=MESH)

    pl.semaphore_wait(barrier, AMP - 1 + 2 * (INT - 1))

    def piece(way, s, j, h):
        hop = 1 if way == RIGHT else -1
        origin = around(-hop * (j - 1))
        rows = pl.ds(64 * h, 64)
        target = gather[s].at[origin, rows, :]
        if j == 1:
            source = slab_ref.at[rows, pl.ds(STARTS[s], WIDTHS[s])]
        else:
            source = target
        k = ((way * 2 + s) * 4 + (j - 1)) * 2 + h
        return pltpu.make_async_remote_copy(
            src_ref=source, dst_ref=target, send_sem=ag_send.at[k], recv_sem=ag_recv.at[k],
            device_id={"amp": d, "int": around(hop)}, device_id_type=MESH,
        )

    started = []

    def launch(way, s, j, h):
        copy = piece(way, s, j, h)
        copy.start()
        started.append(copy)

    def arrived(way, s, j, h):
        hop = 1 if way == RIGHT else -1
        origin = around(-hop * j)
        target = gather[s].at[origin, pl.ds(64 * h, 64), :]
        k = ((way * 2 + s) * 4 + (j - 1)) * 2 + h
        pltpu.make_async_copy(target, target, ag_recv.at[k]).wait()

    def begin(s):
        for h in range(2):
            for way in (RIGHT, LEFT):
                launch(way, s, 1, h)

    def event(s, j, h):
        for way in (RIGHT, LEFT):
            arrived(way, s, j, h)
            if j < 3 or h == way:
                launch(way, s, j + 1, h)

    def last(s):
        arrived(RIGHT, s, 4, 0)
        arrived(LEFT, s, 4, 1)

    def process(s, origin, own):
        a_block = a3[origin]
        start, width = STARTS[s], WIDTHS[s]

        def step(col, n):
            if own:
                b = slab_ref[:, pl.ds(start + col, n)]
            else:
                b = gather[s][origin, :, pl.ds(col, n)]
            high, low = split(b)
            part = mm(a_block, jnp.concatenate([high, high, low], axis=0))
            into = pl.ds(start + col, n)
            if own:
                lad_ref[:, into] = part[:192]
                l2[:, into] = part[192:]
            else:
                lad_ref[:, into] += part[:192]
                l2[:, into] += part[192:]

        full = width // 256

        @pl.loop(0, full)
        def _(i):
            step(pl.multiple_of(i * 256, 256), 256)

        step(full * 256, width - full * 256)

    begin(0)

    here = pl.ds(pl.multiple_of(tile * 128, 128), 128)
    r, c = iota((256, 192), 0), iota((256, 192), 1)
    pick = one_hot((c == 96 * ((r >> 4) & 1) + 12 * (r >> 5) + (r & 15)) & ((r & 15) < 12))
    high, low = split(amp_ref[:, here])
    s_buf[...] = (mm(pick, high) + mm(pick, low)).reshape(INT, 32, 128)

    def s_copy(up):
        return pltpu.make_async_remote_copy(
            src_ref=s_buf.at[up], dst_ref=t_buf.at[z], send_sem=s_sem.at[0], recv_sem=s_sem.at[1],
            device_id={"amp": d, "int": up}, device_id_type=MESH,
        )

    @pl.loop(1, INT)
    def _(j):
        s_copy(lax.rem(z + j, INT)).start()

    t_buf[z] = s_buf[z]

    wpad[...] = jnp.zeros_like(wpad)
    for k in range(12):
        wpad[pl.ds(32 * k, 25), :] = w_ref[k]

    @pl.loop(0, 8)
    def _(i):
        at = pl.ds(pl.multiple_of(i * 128, 128), 128)
        for k4 in range(3):
            wx[core, at, 128 * k4 : 128 * k4 + 128] = wpad[128 * k4 : 128 * k4 + 128, at].T

    w_copy = pltpu.make_async_remote_copy(
        src_ref=wx.at[core], dst_ref=wx.at[core], send_sem=w_sem.at[0], recv_sem=w_sem.at[1],
        device_id={"amp": sibling, "int": z}, device_id_type=MESH,
    )
    w_copy.start()

    seven = pl.ds(0, INT - 1)
    pltpu.make_async_copy(s_buf.at[seven], t_buf.at[seven], s_sem.at[1]).wait()
    r, c = iota((192, 256), 0), iota((192, 256), 1)
    pick = one_hot(c == 32 * ((r >> 1) & 7) + 16 * (r & 1) + (r >> 4))
    high, low = split(t_buf[...].reshape(256, 128))
    u_buf[...] = mm(pick, high) + mm(pick, low)

    @pl.loop(1, 8)
    def _(j):
        pltpu.make_async_remote_copy(
            src_ref=u_buf, dst_ref=v_buf.at[tile], send_sem=u_sem.at[0], recv_sem=u_sem.at[1],
            device_id={"amp": row * 8 + lax.rem(tile + j, 8), "int": z}, device_id_type=MESH,
        ).start()

    v_buf[tile] = u_buf[...]
    event(0, 1, 0)

    for o in range(INT):
        high, low = split(amp_ref[:, 128 * o : 128 * o + 128])
        a3[o, :192, 0:128] = high
        a3[o, :192, 128:256] = low
        a3[o, :192, 256:384] = high

    for n, ref in enumerate(spread):
        @pl.loop(0, ref.shape[0] // 64)
        def _(i):
            c = iota((64, 1024), 0) + (i * 64 - 32 * n)
            l = iota((64, 1024), 1)
            ref[pl.ds(pl.multiple_of(i * 64, 64), 64), :] = one_hot((c == 25 * (l >> 5) + (l & 31)) & ((l & 31) < 25))

    event(0, 1, 1)

    pltpu.make_async_copy(v_buf.at[seven], v_buf.at[seven], u_sem.at[1]).wait()

    @pl.loop(0, INT)
    def _(o):
        high, low = split(v_buf[o])
        a3[o, 192:, 0:128] = high
        a3[o, 192:, 128:256] = low
        a3[o, 192:, 256:384] = high

    event(0, 2, 0)
    process(0, z, True)
    process(0, around(-1), False)
    event(0, 2, 1)
    process(0, around(1), False)
    process(0, around(-2), False)
    event(0, 3, 0)
    process(0, around(2), False)

    w_copy.wait_recv()

    @pl.loop(0, 8)
    def _(i):
        at = pl.ds(pl.multiple_of(i * 128, 128), 128)
        for n in range(2):
            high, low = split(wx[n, at, :])
            whi[at, 384 * n : 384 * n + 384] = high
            wlo[at, 384 * n : 384 * n + 384] = low

    event(0, 3, 1)
    begin(1)
    process(0, around(-3), False)
    process(0, around(3), False)
    last(0)
    process(0, around(4), False)

    def regroup(a):
        win = pl.ds(0, W0) if a == 0 else pl.ds(CUT1, 832)
        size = 896 if a == 0 else 832
        high, low = split(l2[:, win])
        l2h[:, :size] = high
        l2l[:, :size] = low
        lane = iota((16, 128), 1)
        even = (lane & 32) == 0
        lower = (lane & 64) == 0

        @pl.loop(0, 4)
        def _(tp):
            cols = pl.ds(pl.multiple_of(tp * 256, 256), 256)
            table = spread[a][:, cols]
            spaced = mm(l2h[:, :size], table) + mm(l2l[:, :size], table)
            for gg in range(2):
                g = tp * 2 + gg
                for k4 in range(3):
                    x = [spaced[(4 * k4 + q) * 16 : (4 * k4 + q) * 16 + 16, 128 * gg : 128 * gg + 128] for q in range(4)]
                    y = [None] * 4
                    for q in (0, 2):
                        y[q] = jnp.where(even, x[q], pltpu.roll(x[q + 1], 32, 1))
                        y[q + 1] = jnp.where(even, pltpu.roll(x[q], 96, 1), x[q + 1])
                    o = [None] * 4
                    for q in (0, 1):
                        o[q] = jnp.where(lower, y[q], pltpu.roll(y[q + 2], 64, 1))
                        o[q + 2] = jnp.where(lower, pltpu.roll(y[q], 64, 1), y[q + 2])
                    for s in range(4):
                        lanes = pl.ds(384 * (s % 2) + 128 * k4, 128)
                        for hh in range(2):
                            msg[a, 4 * g + 2 * (s // 2) + hh, :, lanes] = o[s][8 * hh : 8 * hh + 8]

        @pl.loop(1, AMP)
        def _(j):
            to = lax.rem(d + j, AMP)
            pltpu.make_async_remote_copy(
                src_ref=msg.at[a, to], dst_ref=rcv.at[a, d], send_sem=a_send.at[a], recv_sem=a_recv.at[a],
                device_id={"amp": to, "int": z}, device_id_type=MESH,
            ).start()

        rcv[a, d] = msg[a, d]

    others = pl.ds(0, AMP - 1)

    def contract(a):
        pltpu.make_async_copy(msg.at[a, others], rcv.at[a, others], a_recv.at[a]).wait()
        r, c = iota((256, 256), 0), iota((256, 256), 1)
        pick = one_hot(c == ((r & 63) >> 1) * 8 + 2 * (r >> 6) + (r & 1))
        high, low = split(rcv[a].reshape(256, 768))
        high = mm(pick, high).astype(BF16)
        low = mm(pick, low).astype(BF16)

        @pl.loop(0, 4)
        def _(q):
            quarter = lax.rem(row + q, 4)
            at = pl.ds(pl.multiple_of(quarter * 256, 256), 256)
            wh, wl = whi[at, :], wlo[at, :]
            part = mm_nt(wh, high) + (mm_nt(wl, high) + mm_nt(wh, low))
            ct[a, pl.ds(quarter * 4, 4)] = part.reshape(4, 64, 256)
            for n in range(4):
                to = quarter * 4 + lax.rem(chip + n, 4)

                @pl.when(to != chip)
                def _():
                    pltpu.make_async_remote_copy(
                        src_ref=ct.at[a, to], dst_ref=rs.at[a, chip], send_sem=r_send.at[a], recv_sem=r_recv.at[a],
                        device_id={"amp": to * 2 + core, "int": z}, device_id_type=MESH,
                    ).start()

        rs[a, chip] = ct[a, chip]

    fifteen = pl.ds(0, 15)

    def narrow(a):
        pltpu.make_async_copy(ct.at[a, fifteen], rs.at[a, fifteen], r_recv.at[a]).wait()
        sxy[...] = rs[a, 0]

        @pl.loop(1, 16)
        def _(n):
            sxy[...] += rs[a, n]

        for cc in range(2):
            for zz in range(4):
                zs[cc * 4 + zz, :, 64 * a : 64 * a + 64] = sxy[32 * cc : 32 * cc + 32, 64 * zz : 64 * zz + 64]

    regroup(0)
    event(1, 1, 0)
    process(1, z, True)
    event(1, 1, 1)
    process(1, around(-1), False)
    process(1, around(1), False)
    event(1, 2, 0)
    event(1, 2, 1)
    contract(0)
    process(1, around(-2), False)
    event(1, 3, 0)
    process(1, around(2), False)
    event(1, 3, 1)
    process(1, around(-3), False)
    process(1, around(3), False)
    last(1)
    process(1, around(4), False)
    regroup(1)
    narrow(0)
    contract(1)
    narrow(1)

    @pl.loop(0, 8)
    def _(n):
        to = chip * 2 + n // 4
        up = core * 4 + lax.rem(n, 4)
        mine = (to == d) & (up == z)

        @pl.when(jnp.logical_not(mine))
        def _():
            pltpu.make_async_remote_copy(
                src_ref=zs.at[n], dst_ref=zr.at[z], send_sem=z_sem.at[0], recv_sem=z_sem.at[1],
                device_id={"amp": to, "int": up}, device_id_type=MESH,
            ).start()

        @pl.when(mine)
        def _():
            zr[z] = zs[n]

    local = core == z // 4

    @pl.when(local)
    def _():
        pltpu.make_async_copy(zs.at[seven], zr.at[seven], z_sem.at[1]).wait()
        pltpu.make_async_copy(zs.at[seven], zr.at[seven], z_sem.at[0]).wait()

    @pl.when(jnp.logical_not(local))
    def _():
        pltpu.make_async_copy(zs, zr, z_sem.at[1]).wait()
        pltpu.make_async_copy(zs, zr, z_sem.at[0]).wait()

    total = zr[0]
    for n in range(1, INT):
        total += zr[n]
    r, c = iota((128, 128), 0), iota((128, 128), 1)
    order = jnp.where(c == 64 * (r & 1) + 2 * ((r & 63) >> 1) + (r >> 6), 1.0, 0.0).astype(F32)
    sum_ref[...] = lax.dot_general(
        order, total, (((1,), (1,)), ((), ())), precision=lax.Precision.HIGHEST, preferred_element_type=F32
    )

    for copy in started:
        copy.wait_send()
    pltpu.make_async_copy(s_buf.at[seven], t_buf.at[seven], s_sem.at[0]).wait()
    pltpu.make_async_copy(v_buf.at[seven], v_buf.at[seven], u_sem.at[0]).wait()
    w_copy.wait_send()
    for a in range(2):
        pltpu.make_async_copy(msg.at[a, others], rcv.at[a, others], a_send.at[a]).wait()
        pltpu.make_async_copy(ct.at[a, fifteen], rs.at[a, fifteen], r_send.at[a]).wait()


def fused(amplitudes, slab_integrals, cycle_integrals):
    vmem = pl.BlockSpec(memory_space=pltpu.VMEM)
    dma = pltpu.SemaphoreType.DMA
    return pl.pallas_call(
        body,
        out_shape=(
            jax.ShapeDtypeStruct((192, 1600), F32),
            jax.ShapeDtypeStruct((128, 32), F32),
        ),
        in_specs=[vmem] * 3,
        out_specs=(vmem, vmem),
        scratch_shapes=[
            pltpu.VMEM((INT, 128, W0), F32),
            pltpu.VMEM((INT, 128, W1), F32),
            pltpu.VMEM((INT, 384, 384), BF16),
            pltpu.VMEM((192, 1600), F32),
            pltpu.VMEM((192, 896), BF16),
            pltpu.VMEM((192, 896), BF16),
            pltpu.VMEM((896, 1024), BF16),
            pltpu.VMEM((832, 1024), BF16),
            pltpu.VMEM((INT, 32, 128), F32),
            pltpu.VMEM((INT, 32, 128), F32),
            pltpu.VMEM((192, 128), F32),
            pltpu.VMEM((INT, 192, 128), F32),
            pltpu.VMEM((384, 1024), F32),
            pltpu.VMEM((2, 1024, 384), F32),
            pltpu.VMEM((1024, 768), BF16),
            pltpu.VMEM((1024, 768), BF16),
            pltpu.VMEM((2, AMP, 8, 768), F32),
            pltpu.VMEM((2, AMP, 8, 768), F32),
            pltpu.VMEM((2, 16, 64, 256), F32),
            pltpu.VMEM((2, 16, 64, 256), F32),
            pltpu.VMEM((64, 256), F32),
            pltpu.VMEM((8, 32, 128), F32),
            pltpu.VMEM((INT, 32, 128), F32),
            dma((32,)),
            dma((32,)),
            dma((2,)),
            dma((2,)),
            dma((2,)),
            dma((2,)),
            dma((2,)),
            dma((2,)),
            dma((2,)),
            dma((2,)),
        ],
        compiler_params=pltpu.CompilerParams(
            collective_id=0, has_side_effects=True, vmem_limit_bytes=58 * 1024 * 1024
        ),
        cost_estimate=pl.CostEstimate(flops=8_000_000_000, bytes_accessed=8_000_000, transcendentals=0),
    )(amplitudes, slab_integrals, cycle_integrals)


def per_device(amplitudes, slab_integrals, cycle_integrals, occ_irrep, vir_irrep):
    ladder, sums = fused(amplitudes, slab_integrals, cycle_integrals)
    i_local = 2
    col_local = sums.shape[1]
    row_start = lax.axis_index("int") * i_local
    batch_labels = lax.dynamic_slice_in_dim(occ_irrep, row_start, i_local, 0)
    slab_labels = vir_irrep[:SLAB]
    row_labels = jnp.bitwise_xor(batch_labels[:, None], slab_labels[None, :]).reshape(-1)
    col_ids = lax.axis_index("amp") * col_local + jnp.arange(col_local, dtype=jnp.int32)
    col_occ = col_ids // SLAB
    col_vir = col_ids % SLAB
    occ_match = col_occ[:, None] == jnp.arange(NOCC, dtype=jnp.int32)[None, :]
    vir_match = col_vir[:, None] == jnp.arange(SLAB, dtype=jnp.int32)[None, :]
    occ_lookup = jnp.sum(jnp.where(occ_match, occ_irrep[None, :], 0), axis=1)
    vir_lookup = jnp.sum(jnp.where(vir_match, slab_labels[None, :], 0), axis=1)
    col_labels = jnp.bitwise_xor(occ_lookup, vir_lookup)
    keep = row_labels[:, None] == col_labels[None, :]
    cycle = jnp.where(keep, sums, jnp.zeros_like(sums))
    return (ladder, cycle)


def solution(mesh):
    in_specs = (P("int", None), P("int", "amp"), P("int", "amp", None), P(), P())
    out_specs = (P("int", "amp"), P("int", "amp"))
    return jax.shard_map(
        per_device, mesh=mesh, in_specs=in_specs, out_specs=out_specs, check_vma=False
    )
```

time: 342 us -> 138 us (0.40); the launches traced: 337 us -> 138 us
  waiting for transfers between devices: 202 us -> 0 us
  Pallas kernels: 0 us -> 128 us
  blocking collectives: 69.3 us -> 0 us
  local copies, waits for them, and re-layouts: 26.2 us -> 6.97 us
  matrix products: 18.3 us -> 0 us
  between operations: 13.8 us -> 0.66 us
  other arithmetic: 6.69 us -> 2.03 us
    pallas_call x0 -> x1, Pallas kernels: none -> 128 us  [fused(): pl.pallas_call(body, out_shape=(jax.ShapeDtypeStruct((192, 1600), F32), j...]
    reduce_scatter x2 -> x0, waiting for transfers between devices: 116 us -> none  [the longest x1 81.4 us: per_device(): lax.psum_scatter(partial_value, 'amp', scatter_dimension=1, tiled=True)]
    all_gather x1 -> x0, waiting for transfers between devices: 86.1 us -> none  [per_device(): lax.all_gather(slab_integrals, 'int', axis=0, tiled=True)]
    all_to_all x2 -> x0, blocking collectives: 69.3 us -> none  [the longest x1 35.3 us: per_device(): lax.all_to_all(lax.all_to_all(blocks, 'amp', split_axis=3, concat_axis=2,...]
    dot_general x2 -> x0, matrix products: 18.3 us -> none  [the longest x1 10 us: per_device(): jnp.dot(amplitudes, lax.all_gather(slab_integrals, 'int', axis=0, tiled=T...]
    all_to_all x4 -> x0, local copies, waits for them, and re-layouts: 8.63 us -> none  [the longest x2 4.48 us: per_device(): lax.all_to_all(lax.all_to_all(blocks, 'amp', split_axis=3, concat_axis=2,...]
    reshape x2 -> x0, local copies, waits for them, and re-layouts: 6.37 us -> none  [per_device(): blocks = ladder.reshape(i_local, NOCC, a_local, NVIR)]
    all_to_all x1 -> x0, other arithmetic: 4.85 us -> none  [per_device(): lax.all_to_all(lax.all_to_all(blocks, 'amp', split_axis=3, concat_axis=2,...]
  transfers between devices with their start and end apart: 3 -> 0, of which waited for: 3 -> 0; matrix products, arithmetic and copies ran while one was open for 0% -> 0% of each run, Pallas kernels for 0% -> 0%
where the time goes in v1:
time: 138 us
  Pallas kernels  128 us (93%)
  local copies, waits for them, and re-layouts  6.97 us (5%)
  other arithmetic  2.03 us (1%)
    pallas_call x1, Pallas kernels, fused(): pl.pallas_call(body, out_shape=(jax.ShapeDtypeStruct((192, 1600), F32), j...  128 us
    unnamed x3, local copies, waits for them, and re-layouts  5.46 us

profile of v1, /device:TPU:1, one launch (start us, length us, event | category | flops | bytes accessed | tf_op | source)
XLA Modules:
  0.0 137.7 jit_solution(12050975848199199815)
XLA Ops:
  0.6 0.7 dynamic_slice.3
  1.4 0.7 slice.3
  2.1 0.1 broadcast_xor_fusion
  2.1 0.1 xor.30
  2.2 0.2 select_reduce_fusion
  2.4 0.8 select_reduce_fusion.1
  3.3 2.4 %copy.9.slab_ref = f32[128,1600]{1,0:T(8,128)} copy(f32[128,1600]{0,1:T(8,128)} %param.6) | data formatting | bytes 1638400 | tf_op args[1]
  5.6 128.0 %shard_map.68 = (f32[192,1600]{1,0:T(8,128)}, f32[128,32]{1,0:T(8,128)}) custom-call(f32[192,1024]{1,0:T(8,128)} %amp_ref.1, f32[128,1600]{1,0:T(8,128)} %copy.9.slab_ref, f32[12,25,1024]{2,1,0:T(8,128)} %w_ref.1), custom_call_target="tpu_custom_call" | custom-call | flops 8000000000 | bytes 8000000 | tf_op jit(solution)/shard_map/pallas_call | solution.py:412
  133.6 0.9 compare_select_fusion
  134.6 0.7 copy.10
  135.3 2.4 %copy.12 = f32[192,1600]{1,0:T(8,128)} copy(f32[192,1600]{1,0:T(8,128)} %get-tuple-element.14) | data formatting | bytes 2457600
  (2 shorter events, 0.0 us)

commit v2 on v0

v2 whole, which is shorter than its diff:
```python
import jax
import jax.numpy as jnp
from jax import lax
from jax.experimental import pallas as pl
from jax.experimental.pallas import tpu as pltpu
from jax.sharding import PartitionSpec as P

F32 = jnp.float32
BF16 = jnp.bfloat16
MESH = pl.DeviceIdType.MESH

INT = 8
ROW = 8
COL = 4
WIDTHS = (800, 400, 400)
STARTS = (0, 800, 1200)
RIGHT, LEFT = 0, 1


def iota(shape, dim):
    return lax.broadcasted_iota(jnp.int32, shape, dim)


def split(x):
    high = x.astype(BF16)
    return high, (x - high.astype(F32)).astype(BF16)


def mm(a, b):
    return jnp.dot(a, b, preferred_element_type=F32)


def mm_nt(a, b):
    return lax.dot_general(a, b, (((1,), (1,)), ((), ())), preferred_element_type=F32)


def one_hot(match):
    return jnp.where(match, 1.0, 0.0).astype(BF16)


def body(
    amp_hbm, slab_hbm, w_hbm, occ_ref, vir_ref,
    lad_hbm, sum_ref,
    amp_ref, w_ref, lad_ref, slab, a3, acc0, acc1, acc2, table, s_buf, t_buf, u_buf, v_buf,
    wg, wpad, whi, wlo, msg, rcv, ct, rs, zs, zr, ys, yr, mask,
    in_sem, out_sem, ag_send, ag_recv, s_sem, u_sem, w_send, w_recv, a_send, a_recv, r_send, r_recv, z_sem, y_sem,
):
    d = lax.axis_index("amp")
    z = lax.axis_index("int")
    y = d // ROW
    xc = lax.rem(d, ROW)
    accs = (acc0, acc1, acc2)

    def around(step):
        return lax.rem(z + step + INT, INT)

    def in_row(j):
        return {"amp": y * ROW + lax.rem(xc + j, ROW), "int": z}

    def in_col(j):
        return {"amp": lax.rem(y + j, COL) * ROW + xc, "int": z}

    def in_stack(j):
        return {"amp": d, "int": lax.rem(z + j, INT)}

    barrier = pltpu.get_barrier_semaphore()

    @pl.loop(1, 8)
    def _(j):
        pl.semaphore_signal(barrier, inc=1, device_id=in_row(j), device_id_type=MESH)
        pl.semaphore_signal(barrier, inc=1, device_id=in_stack(j), device_id_type=MESH)

    @pl.loop(1, COL)
    def _(j):
        pl.semaphore_signal(barrier, inc=1, device_id=in_col(j), device_id_type=MESH)

    load_amp = pltpu.make_async_copy(amp_hbm, amp_ref, in_sem.at[0])
    load_slab = pltpu.make_async_copy(slab_hbm, slab.at[z], in_sem.at[1])
    load_w = pltpu.make_async_copy(w_hbm, w_ref, in_sem.at[2])
    load_amp.start()
    load_slab.start()
    load_w.start()

    def place(c, h):
        half = WIDTHS[c] // 2
        return pl.ds(STARTS[c] + half * h, half)

    def piece(way, c, j, h):
        hop = 1 if way == RIGHT else -1
        part = slab.at[around(-hop * (j - 1)), place(c, h), :]
        k = ((way * 3 + c) * 4 + (j - 1)) * 2 + h
        return pltpu.make_async_remote_copy(
            src_ref=part, dst_ref=part, send_sem=ag_send.at[k], recv_sem=ag_recv.at[k],
            device_id={"amp": d, "int": around(hop)}, device_id_type=MESH,
        )

    started = []

    def launch(way, c, j, h):
        copy = piece(way, c, j, h)
        copy.start()
        started.append(copy)

    def arrived(way, c, j, h):
        hop = 1 if way == RIGHT else -1
        part = slab.at[around(-hop * j), place(c, h), :]
        k = ((way * 3 + c) * 4 + (j - 1)) * 2 + h
        pltpu.make_async_copy(part, part, ag_recv.at[k]).wait()

    def begin(c):
        for h in range(2):
            for way in (RIGHT, LEFT):
                launch(way, c, 1, h)

    def event(c, j, h):
        for way in (RIGHT, LEFT):
            arrived(way, c, j, h)
            if j < 3 or h == way:
                launch(way, c, j + 1, h)

    def last(c):
        arrived(RIGHT, c, 4, 0)
        arrived(LEFT, c, 4, 1)

    def process(c, step):
        origin = around(step)
        a_block = a3[origin]
        tiles = ((0, 512), (512, 288)) if c == 0 else ((0, 400),)
        for col, n in tiles:
            high, low = split(slab[origin, STARTS[c] + col : STARTS[c] + col + n, :])
            part = mm_nt(a_block, jnp.concatenate([high, high, low], axis=1))
            if step == 0:
                accs[c][:, col : col + n] = part
            else:
                accs[c][:, col : col + n] += part

    load_amp.wait()
    here = pl.ds(pl.multiple_of(xc * 128, 128), 128)
    r, c = iota((256, 192), 0), iota((256, 192), 1)
    pick = one_hot((c == 96 * ((r >> 4) & 1) + 12 * (r >> 5) + (r & 15)) & ((r & 15) < 12))
    high, low = split(amp_ref[:, here])
    s_buf[...] = (mm(pick, high) + mm(pick, low)).reshape(INT, 32, 128)
    load_slab.wait()
    pl.semaphore_wait(barrier, 7 + 7 + 3)

    @pl.loop(1, INT)
    def _(j):
        up = lax.rem(z + j, INT)
        pltpu.make_async_remote_copy(
            src_ref=s_buf.at[up], dst_ref=t_buf.at[z], send_sem=s_sem.at[0], recv_sem=s_sem.at[1],
            device_id=in_stack(j), device_id_type=MESH,
        ).start()

    begin(0)
    t_buf[z] = s_buf[z]

    load_w.wait()
    for k in range(12):
        wg[y, 25 * k : 25 * k + 25, :] = w_ref[k]
    wg[y, 300:304, :] = jnp.zeros((4, 1024), F32)

    def w_piece(way, h, hop_from):
        hop = 1 if way == RIGHT else 3
        part = wg.at[lax.rem(y + (4 - hop) * hop_from, COL), pl.ds(152 * h, 152), :]
        k = way * 3 + (2 if hop_from else h)
        return pltpu.make_async_remote_copy(
            src_ref=part, dst_ref=part, send_sem=w_send.at[k], recv_sem=w_recv.at[k],
            device_id=in_col(hop), device_id_type=MESH,
        )

    def w_arrived(way, h, hops):
        hop = 1 if way == RIGHT else 3
        part = wg.at[lax.rem(y + (4 - hop) * hops, COL), pl.ds(152 * h, 152), :]
        pltpu.make_async_copy(part, part, w_recv.at[way * 3 + (2 if hops == 2 else h)]).wait()

    def w_launch(*which):
        copy = w_piece(*which)
        copy.start()
        started.append(copy)

    w_launch(RIGHT, 0, 0)
    w_launch(LEFT, 1, 0)
    w_launch(RIGHT, 1, 0)
    w_launch(LEFT, 0, 0)

    seven = pl.ds(0, 7)
    pltpu.make_async_copy(s_buf.at[seven], t_buf.at[seven], s_sem.at[1]).wait()
    r, c = iota((192, 256), 0), iota((192, 256), 1)
    pick = one_hot(c == 32 * ((r >> 1) & 7) + 16 * (r & 1) + (r >> 4))
    high, low = split(t_buf[...].reshape(256, 128))
    u_buf[...] = mm(pick, high) + mm(pick, low)

    @pl.loop(1, ROW)
    def _(j):
        pltpu.make_async_remote_copy(
            src_ref=u_buf, dst_ref=v_buf.at[xc], send_sem=u_sem.at[0], recv_sem=u_sem.at[1],
            device_id=in_row(j), device_id_type=MESH,
        ).start()

    v_buf[xc] = u_buf[...]

    r, c = iota((400, 512), 0), iota((400, 512), 1)
    table[...] = one_hot((r == 200 * (c >> 8) + 25 * ((c >> 5) & 7) + (c & 31)) & ((c & 31) < 25))

    sub, lane = iota((32, 128), 0), iota((32, 128), 1)
    row_label = jnp.where(lane < 64, occ_ref[2 * z], occ_ref[2 * z + 1])
    col_label = jnp.zeros((32, 128), jnp.int32) + occ_ref[d // 2]
    first = 32 * lax.rem(d, 2)

    def label_step(b, both):
        rows, cols = both
        rows = jnp.where((lane & 63) == b, rows ^ vir_ref[b], rows)
        cols = jnp.where(sub + first == b, cols ^ vir_ref[b], cols)
        return rows, cols

    row_label, col_label = lax.fori_loop(0, 64, label_step, (row_label, col_label))
    mask[...] = jnp.where(row_label == col_label, 1.0, 0.0).astype(F32)

    for o in range(INT):
        high, low = split(amp_ref[:, 128 * o : 128 * o + 128])
        a3[o, :192, 0:128] = high
        a3[o, :192, 128:256] = low
        a3[o, :192, 256:384] = high

    wpad[...] = jnp.zeros_like(wpad)

    def w_step(block):
        for k in range(12):
            wpad[32 * k : 32 * k + 25, :] = wg[block, 25 * k : 25 * k + 25, :]
        into = block // 2
        lanes = lax.rem(block, 2) * 384

        @pl.loop(0, 8)
        def _(i):
            at = pl.ds(pl.multiple_of(i * 128, 128), 128)
            for k4 in range(3):
                high, low = split(wpad[128 * k4 : 128 * k4 + 128, at].T)
                to = pl.ds(pl.multiple_of(lanes + 128 * k4, 128), 128)
                whi[into, at, to] = high
                wlo[into, at, to] = low

    event(0, 1, 0)
    w_step(y)
    event(0, 1, 1)
    event(0, 2, 0)
    pltpu.make_async_copy(v_buf.at[seven], v_buf.at[seven], u_sem.at[1]).wait()

    @pl.loop(0, INT)
    def _(o):
        high, low = split(v_buf[o])
        a3[o, 192:, 0:128] = high
        a3[o, 192:, 128:256] = low
        a3[o, 192:, 256:384] = high

    w_arrived(RIGHT, 0, 1)
    w_launch(RIGHT, 0, 1)
    w_arrived(LEFT, 1, 1)
    w_launch(LEFT, 1, 1)
    process(0, 0)
    process(0, -1)
    event(0, 2, 1)
    process(0, 1)
    process(0, -2)
    event(0, 3, 0)
    begin(1)
    process(0, 2)
    event(0, 3, 1)
    process(0, -3)
    process(0, 3)
    last(0)
    process(0, 4)

    def regroup(a, half):
        source = acc0[192:, 400 * half : 400 * half + 400] if a == 0 else accs[1 + half][192:, :]
        high, low = split(source)
        spaced = mm(high, table[...]) + mm(low, table[...])
        lane = iota((16, 128), 1)
        even = (lane & 32) == 0
        lower = (lane & 64) == 0
        for t in range(4):
            for k4 in range(3):
                x = [spaced[(4 * k4 + q) * 16 : (4 * k4 + q) * 16 + 16, 128 * t : 128 * t + 128] for q in range(4)]
                v = [None] * 4
                for q in (0, 2):
                    v[q] = jnp.where(even, x[q], pltpu.roll(x[q + 1], 32, 1))
                    v[q + 1] = jnp.where(even, pltpu.roll(x[q], 96, 1), x[q + 1])
                o = [None] * 4
                for q in (0, 1):
                    o[q] = jnp.where(lower, v[q], pltpu.roll(v[q + 2], 64, 1))
                    o[q + 2] = jnp.where(lower, pltpu.roll(v[q], 64, 1), v[q + 2])
                at = 384 * (t // 2) + 128 * k4
                for s in range(4):
                    msg[a, half, 4 * (t % 2) + s, :, at : at + 128] = o[s]

        @pl.loop(1, ROW)
        def _(j):
            to = lax.rem(xc + j, ROW)
            pltpu.make_async_remote_copy(
                src_ref=msg.at[a, half, to], dst_ref=rcv.at[a, half, xc],
                send_sem=a_send.at[2 * a + half], recv_sem=a_recv.at[2 * a + half],
                device_id=in_row(j), device_id_type=MESH,
            ).start()

        rcv[a, half, xc] = msg[a, half, xc]

    def contract(a, half):
        pltpu.make_async_copy(
            msg.at[a, half, seven], rcv.at[a, half, seven], a_recv.at[2 * a + half]
        ).wait()
        r, c = iota((128, 128), 0), iota((128, 128), 1)
        pick = one_hot(c == (r & 7) * 16 + 2 * (r >> 4) + ((r >> 3) & 1))
        high, low = split(rcv[a, half].reshape(128, 768))
        high = mm(pick, high).astype(BF16)
        low = mm(pick, low).astype(BF16)
        both = jnp.concatenate([high, low], axis=0)

        @pl.loop(0, COL)
        def _(q):
            at = pl.ds(pl.multiple_of(q * 256, 256), 256)
            part = mm_nt(whi[half, at, :], both)
            part = part[:, :128] + (part[:, 128:] + mm_nt(wlo[half, at, :], high))
            part = part.reshape(ROW, 32, 128)
            if half == 0:
                ct[a, :, q] = part
            else:
                ct[a, :, q] += part

        if half == 1:
            @pl.loop(1, ROW)
            def _(j):
                to = lax.rem(xc + j, ROW)
                pltpu.make_async_remote_copy(
                    src_ref=ct.at[a, to], dst_ref=rs.at[a, xc], send_sem=r_send.at[a], recv_sem=r_recv.at[a],
                    device_id=in_row(j), device_id_type=MESH,
                ).start()

            rs[a, xc] = ct[a, xc]

    def narrow(a):
        pltpu.make_async_copy(ct.at[a, seven], rs.at[a, seven], r_recv.at[a]).wait()
        total = rs[a, 0]
        for n in range(1, ROW):
            total += rs[a, n]
        zs[:, 16 * a : 16 * a + 16, :] = total.reshape(128, 128).T.reshape(INT, 16, 128)

    def w_rest(way, halves):
        for h in halves:
            w_arrived(way, h, 1)

    regroup(0, 0)
    regroup(0, 1)
    event(1, 1, 0)
    lad_ref[:, 0:800] = acc0[:192, :]
    event(1, 1, 1)
    store_0 = pltpu.make_async_copy(lad_ref.at[:, pl.ds(0, 768)], lad_hbm.at[:, pl.ds(0, 768)], out_sem.at[0])
    store_0.start()
    process(1, 0)
    process(1, -1)
    event(1, 2, 0)
    w_rest(RIGHT, (1,))
    w_step(lax.rem(y + 3, COL))
    event(1, 2, 1)
    begin(2)
    w_rest(LEFT, (0,))
    w_step(lax.rem(y + 1, COL))
    event(1, 3, 0)
    process(1, 1)
    process(1, -2)
    event(1, 3, 1)
    process(1, 2)
    process(1, -3)
    process(1, 3)
    last(1)
    process(1, 4)
    regroup(1, 0)
    event(2, 1, 0)
    w_arrived(RIGHT, 0, 2)
    w_arrived(LEFT, 1, 2)
    w_step(lax.rem(y + 2, COL))
    event(2, 1, 1)
    contract(0, 0)
    event(2, 2, 0)
    contract(0, 1)
    event(2, 2, 1)
    process(2, 0)
    process(2, -1)
    process(2, 1)
    event(2, 3, 0)
    contract(1, 0)
    event(2, 3, 1)
    process(2, -2)
    process(2, 2)
    process(2, -3)
    process(2, 3)
    last(2)
    process(2, 4)
    regroup(1, 1)
    lad_ref[:, 800:1200] = acc1[:192, :]
    lad_ref[:, 1200:1600] = acc2[:192, :]
    store_1 = pltpu.make_async_copy(lad_ref.at[:, pl.ds(768, 832)], lad_hbm.at[:, pl.ds(768, 832)], out_sem.at[1])
    store_1.start()
    narrow(0)
    contract(1, 1)
    narrow(1)

    @pl.loop(1, INT)
    def _(j):
        up = lax.rem(z + j, INT)
        pltpu.make_async_remote_copy(
            src_ref=zs.at[up], dst_ref=zr.at[z], send_sem=z_sem.at[0], recv_sem=z_sem.at[1],
            device_id=in_stack(j), device_id_type=MESH,
        ).start()

    zr[z] = zs[z]
    pltpu.make_async_copy(zs.at[seven], zr.at[seven], z_sem.at[1]).wait()
    total = zr[0]
    for n in range(1, INT):
        total += zr[n]
    ys[...] = total

    @pl.loop(1, COL)
    def _(j):
        pltpu.make_async_remote_copy(
            src_ref=ys, dst_ref=yr.at[y], send_sem=y_sem.at[0], recv_sem=y_sem.at[1],
            device_id=in_col(j), device_id_type=MESH,
        ).start()

    yr[y] = total
    three = pl.ds(0, 3)
    pltpu.make_async_copy(yr.at[three], yr.at[three], y_sem.at[1]).wait()
    exact = dict(precision=lax.Precision.HIGHEST, preferred_element_type=F32)
    nt = (((1,), (1,)), ((), ()))
    r, c = iota((32, 128), 0), iota((32, 128), 1)
    mine = jnp.where(c == 32 * y + r, 1.0, 0.0).astype(F32)
    kept = lax.dot_general(mine, yr[...].reshape(128, 128), nt, **exact)
    r, c = iota((128, 128), 0), iota((128, 128), 1)
    order = (r == 32 * ((c >> 4) & 3) + 16 * (c & 1) + 8 * (c >> 6) + ((c >> 1) & 7))
    kept = jnp.dot(kept, jnp.where(order, 1.0, 0.0).astype(F32), **exact)
    sum_ref[...] = jnp.where(mask[...] > 0.5, kept, jnp.zeros_like(kept))

    for copy in started:
        copy.wait_send()
    pltpu.make_async_copy(s_buf.at[seven], t_buf.at[seven], s_sem.at[0]).wait()
    pltpu.make_async_copy(v_buf.at[seven], v_buf.at[seven], u_sem.at[0]).wait()
    for a in range(2):
        for half in range(2):
            pltpu.make_async_copy(
                msg.at[a, half, seven], rcv.at[a, half, seven], a_send.at[2 * a + half]
            ).wait()
        pltpu.make_async_copy(ct.at[a, seven], rs.at[a, seven], r_send.at[a]).wait()
    pltpu.make_async_copy(zs.at[seven], zr.at[seven], z_sem.at[0]).wait()
    pltpu.make_async_copy(yr.at[three], yr.at[three], y_sem.at[0]).wait()
    store_0.wait()
    store_1.wait()


def per_device(amplitudes, slab_integrals, cycle_integrals, occ_irrep, vir_irrep):
    vmem = pl.BlockSpec(memory_space=pltpu.VMEM)
    smem = pl.BlockSpec(memory_space=pltpu.SMEM)
    anywhere = pl.BlockSpec(memory_space=pl.ANY)
    dma = pltpu.SemaphoreType.DMA
    ladder, sums = pl.pallas_call(
        body,
        out_shape=(
            jax.ShapeDtypeStruct((192, 1600), F32),
            jax.ShapeDtypeStruct((32, 128), F32),
        ),
        in_specs=[anywhere] * 3 + [smem] * 2,
        out_specs=(anywhere, vmem),
        scratch_shapes=[
            pltpu.VMEM((192, 1024), F32),
            pltpu.VMEM((12, 25, 1024), F32),
            pltpu.VMEM((192, 1600), F32),
            pltpu.VMEM((INT, 1600, 128), F32),
            pltpu.VMEM((INT, 384, 384), BF16),
            pltpu.VMEM((384, 800), F32),
            pltpu.VMEM((384, 400), F32),
            pltpu.VMEM((384, 400), F32),
            pltpu.VMEM((400, 512), BF16),
            pltpu.VMEM((INT, 32, 128), F32),
            pltpu.VMEM((INT, 32, 128), F32),
            pltpu.VMEM((192, 128), F32),
            pltpu.VMEM((INT, 192, 128), F32),
            pltpu.VMEM((COL, 304, 1024), F32),
            pltpu.VMEM((384, 1024), F32),
            pltpu.VMEM((2, 1024, 768), BF16),
            pltpu.VMEM((2, 1024, 768), BF16),
            pltpu.VMEM((2, 2, ROW, 16, 768), F32),
            pltpu.VMEM((2, 2, ROW, 16, 768), F32),
            pltpu.VMEM((2, ROW, COL, 32, 128), F32),
            pltpu.VMEM((2, ROW, COL, 32, 128), F32),
            pltpu.VMEM((INT, 32, 128), F32),
            pltpu.VMEM((INT, 32, 128), F32),
            pltpu.VMEM((32, 128), F32),
            pltpu.VMEM((COL, 32, 128), F32),
            pltpu.VMEM((32, 128), F32),
            dma((3,)),
            dma((2,)),
            dma((48,)),
            dma((48,)),
            dma((2,)),
            dma((2,)),
            dma((6,)),
            dma((6,)),
            dma((4,)),
            dma((4,)),
            dma((2,)),
            dma((2,)),
            dma((2,)),
            dma((2,)),
        ],
        compiler_params=pltpu.CompilerParams(
            collective_id=0, has_side_effects=True, vmem_limit_bytes=58 * 1024 * 1024
        ),
        cost_estimate=pl.CostEstimate(flops=8_000_000_000, bytes_accessed=8_000_000, transcendentals=0),
    )(amplitudes, slab_integrals.T, cycle_integrals, occ_irrep, vir_irrep)
    return ladder, sums.T


def solution(mesh):
    in_specs = (P("int", None), P("int", "amp"), P("int", "amp", None), P(), P())
    out_specs = (P("int", "amp"), P("int", "amp"))
    return jax.shard_map(
        per_device, mesh=mesh, in_specs=in_specs, out_specs=out_specs, check_vma=False
    )
```

time: 342 us -> 117 us (0.34); the launches traced: 337 us -> 117 us
  waiting for transfers between devices: 202 us -> 0 us
  Pallas kernels: 0 us -> 113 us
  blocking collectives: 69.3 us -> 0 us
  local copies, waits for them, and re-layouts: 26.2 us -> 3.05 us
  matrix products: 18.3 us -> 0 us
  between operations: 13.8 us -> 0.65 us
  other arithmetic: 6.69 us -> 0 us
    reduce_scatter x2 -> x0, waiting for transfers between devices: 116 us -> none  [the longest x1 81.4 us: per_device(): lax.psum_scatter(partial_value, 'amp', scatter_dimension=1, tiled=True)]
    pallas_call x0 -> x1, Pallas kernels: none -> 113 us  [per_device(): pl.pallas_call(body, out_shape=(jax.ShapeDtypeStruct((192, 1600), F32), j...]
    all_gather x1 -> x0, waiting for transfers between devices: 86.1 us -> none  [per_device(): lax.all_gather(slab_integrals, 'int', axis=0, tiled=True)]
    all_to_all x2 -> x0, blocking collectives: 69.3 us -> none  [the longest x1 35.3 us: per_device(): lax.all_to_all(lax.all_to_all(blocks, 'amp', split_axis=3, concat_axis=2,...]
    dot_general x2 -> x0, matrix products: 18.3 us -> none  [the longest x1 10 us: per_device(): jnp.dot(amplitudes, lax.all_gather(slab_integrals, 'int', axis=0, tiled=T...]
    all_to_all x4 -> x0, local copies, waits for them, and re-layouts: 8.63 us -> none  [the longest x2 4.48 us: per_device(): lax.all_to_all(lax.all_to_all(blocks, 'amp', split_axis=3, concat_axis=2,...]
    reshape x2 -> x0, local copies, waits for them, and re-layouts: 6.37 us -> none  [per_device(): blocks = ladder.reshape(i_local, NOCC, a_local, NVIR)]
    unnamed x8 -> x4, local copies, waits for them, and re-layouts: 8.11 us -> 3.05 us
  transfers between devices with their start and end apart: 3 -> 0, of which waited for: 3 -> 0; matrix products, arithmetic and copies ran while one was open for 0% -> 0% of each run, Pallas kernels for 0% -> 0%
where the time goes in v2:
time: 117 us
  Pallas kernels  113 us (97%)
  local copies, waits for them, and re-layouts  3.05 us (3%)
    pallas_call x1, Pallas kernels, per_device(): pl.pallas_call(body, out_shape=(jax.ShapeDtypeStruct((192, 1600), F32), j...  113 us
    unnamed x4, local copies, waits for them, and re-layouts  3.05 us

profile of v2, /device:TPU:1, one launch (start us, length us, event | category | flops | bytes accessed | tf_op | source)
XLA Modules:
  0.0 116.9 jit_solution(14159180874093073302)
XLA Ops:
  0.6 113.2 %shard_map.68 = (f32[192,1600]{1,0:T(8,128)}, f32[32,128]{1,0:T(8,128)}) custom-call(f32[192,1024]{1,0:T(8,128)} %amp_hbm.1, f32[1600,128]{1,0:T(8,128)} %bitcast.3, f32[12,25,1024]{2,1,0:T(8,128)} %w_hbm.1, s32[96]{0:T(128)} %occ_ref.1, s32[800]{0:T(1024)} %vir_ref.1), custom_call_target="tpu_custom_call" | custom-call | flops 8000000000 | bytes 8000000 | tf_op jit(solution)/shard_map/pallas_call | solution.py:462
  113.9 0.0 copy-start
  113.9 2.4 %copy.9 = f32[192,1600]{1,0:T(8,128)} copy(f32[192,1600]{1,0:T(8,128)} %get-tuple-element.8) | data formatting | bytes 2457600
  116.3 0.0 copy-done
  116.3 0.6 copy.10
Async XLA Ops:
  113.9 2.5 %copy-start = (f32[32,128]{1,0:T(8,128)S(1)}, f32[32,128]{1,0:T(8,128)}, u32[]{:S(2)}) copy-start(f32[32,128]{1,0:T(8,128)} %get-tuple-element.5) | copy-start | bytes 49156

commit v3 on v2

--- a/solution.py
+++ b/solution.py
@@ -12,8 +12,13 @@
 INT = 8
 ROW = 8
 COL = 4
+PLANE = ROW * COL
 WIDTHS = (800, 400, 400)
 STARTS = (0, 800, 1200)
+PIECES = tuple(
+    tuple((start + width * q // 4 // 8 * 8, (width * (q + 1) // 4 // 8 - width * q // 4 // 8) * 8) for q in range(4))
+    for start, width in zip(STARTS, WIDTHS)
+)
 RIGHT, LEFT = 0, 1
 
 
@@ -42,8 +47,8 @@
     amp_hbm, slab_hbm, w_hbm, occ_ref, vir_ref,
     lad_hbm, sum_ref,
     amp_ref, w_ref, lad_ref, slab, a3, acc0, acc1, acc2, table, s_buf, t_buf, u_buf, v_buf,
-    wg, wpad, whi, wlo, msg, rcv, ct, rs, zs, zr, ys, yr, mask,
-    in_sem, out_sem, ag_send, ag_recv, s_sem, u_sem, w_send, w_recv, a_send, a_recv, r_send, r_recv, z_sem, y_sem,
+    wg, wpad, whi, wlo, msg, rcv, ct, rs, zs, zr, mask,
+    in_sem, out_sem, ag_send, ag_recv, s_sem, u_sem, w_send, w_recv, a_send, a_recv, r_send, r_recv, z_sem,
 ):
     d = lax.axis_index("amp")
     z = lax.axis_index("int")
@@ -65,14 +70,13 @@
 
     barrier = pltpu.get_barrier_semaphore()
 
-    @pl.loop(1, 8)
+    @pl.loop(1, PLANE)
     def _(j):
-        pl.semaphore_signal(barrier, inc=1, device_id=in_row(j), device_id_type=MESH)
+        pl.semaphore_signal(barrier, inc=1, device_id={"amp": lax.rem(d + j, PLANE), "int": z}, device_id_type=MESH)
+
+    @pl.loop(1, INT)
+    def _(j):
         pl.semaphore_signal(barrier, inc=1, device_id=in_stack(j), device_id_type=MESH)
-
-    @pl.loop(1, COL)
-    def _(j):
-        pl.semaphore_signal(barrier, inc=1, device_id=in_col(j), device_id_type=MESH)
 
     load_amp = pltpu.make_async_copy(amp_hbm, amp_ref, in_sem.at[0])
     load_slab = pltpu.make_async_copy(slab_hbm, slab.at[z], in_sem.at[1])
@@ -81,14 +85,13 @@
     load_slab.start()
     load_w.start()
 
-    def place(c, h):
-        half = WIDTHS[c] // 2
-        return pl.ds(STARTS[c] + half * h, half)
-
-    def piece(way, c, j, h):
+    def place(c, q):
+        return pl.ds(*PIECES[c][q])
+
+    def piece(way, c, j, q):
         hop = 1 if way == RIGHT else -1
-        part = slab.at[around(-hop * (j - 1)), place(c, h), :]
-        k = ((way * 3 + c) * 4 + (j - 1)) * 2 + h
+        part = slab.at[around(-hop * (j - 1)), place(c, q), :]
+        k = ((way * 3 + c) * 4 + (j - 1)) * 4 + q
         return pltpu.make_async_remote_copy(
             src_ref=part, dst_ref=part, send_sem=ag_send.at[k], recv_sem=ag_recv.at[k],
             device_id={"amp": d, "int": around(hop)}, device_id_type=MESH,
@@ -96,31 +99,32 @@
 
     started = []
 
-    def launch(way, c, j, h):
-        copy = piece(way, c, j, h)
+    def launch(way, c, j, q):
+        copy = piece(way, c, j, q)
         copy.start()
         started.append(copy)
 
-    def arrived(way, c, j, h):
+    def arrived(way, c, j, q):
         hop = 1 if way == RIGHT else -1
-        part = slab.at[around(-hop * j), place(c, h), :]
-        k = ((way * 3 + c) * 4 + (j - 1)) * 2 + h
+        part = slab.at[around(-hop * j), place(c, q), :]
+        k = ((way * 3 + c) * 4 + (j - 1)) * 4 + q
         pltpu.make_async_copy(part, part, ag_recv.at[k]).wait()
 
+    order = ((RIGHT, 0), (LEFT, 3), (RIGHT, 1), (LEFT, 2)), ((RIGHT, 2), (LEFT, 1), (RIGHT, 3), (LEFT, 0))
+
     def begin(c):
-        for h in range(2):
-            for way in (RIGHT, LEFT):
-                launch(way, c, 1, h)
-
-    def event(c, j, h):
-        for way in (RIGHT, LEFT):
-            arrived(way, c, j, h)
-            if j < 3 or h == way:
-                launch(way, c, j + 1, h)
+        for way, q in order[0] + order[1]:
+            launch(way, c, 1, q)
+
+    def event(c, j, g):
+        for way, q in order[g]:
+            arrived(way, c, j, q)
+            if j < 3 or g == 0:
+                launch(way, c, j + 1, q)
 
     def last(c):
-        arrived(RIGHT, c, 4, 0)
-        arrived(LEFT, c, 4, 1)
+        for way, q in order[0]:
+            arrived(way, c, 4, q)
 
     def process(c, step):
         origin = around(step)
@@ -141,7 +145,7 @@
     high, low = split(amp_ref[:, here])
     s_buf[...] = (mm(pick, high) + mm(pick, low)).reshape(INT, 32, 128)
     load_slab.wait()
-    pl.semaphore_wait(barrier, 7 + 7 + 3)
+    pl.semaphore_wait(barrier, PLANE - 1 + INT - 1)
 
     @pl.loop(1, INT)
     def _(j):
@@ -184,20 +188,6 @@
     w_launch(LEFT, 0, 0)
 
     seven = pl.ds(0, 7)
-    pltpu.make_async_copy(s_buf.at[seven], t_buf.at[seven], s_sem.at[1]).wait()
-    r, c = iota((192, 256), 0), iota((192, 256), 1)
-    pick = one_hot(c == 32 * ((r >> 1) & 7) + 16 * (r & 1) + (r >> 4))
-    high, low = split(t_buf[...].reshape(256, 128))
-    u_buf[...] = mm(pick, high) + mm(pick, low)
-
-    @pl.loop(1, ROW)
-    def _(j):
-        pltpu.make_async_remote_copy(
-            src_ref=u_buf, dst_ref=v_buf.at[xc], send_sem=u_sem.at[0], recv_sem=u_sem.at[1],
-            device_id=in_row(j), device_id_type=MESH,
-        ).start()
-
-    v_buf[xc] = u_buf[...]
 
     r, c = iota((400, 512), 0), iota((400, 512), 1)
     table[...] = one_hot((r == 200 * (c >> 8) + 25 * ((c >> 5) & 7) + (c & 31)) & ((c & 31) < 25))
@@ -240,9 +230,28 @@
                 wlo[into, at, to] = low
 
     event(0, 1, 0)
+    pltpu.make_async_copy(s_buf.at[seven], t_buf.at[seven], s_sem.at[1]).wait()
+    r, c = iota((192, 256), 0), iota((192, 256), 1)
+    pick = one_hot(c == 32 * ((r >> 1) & 7) + 16 * (r & 1) + (r >> 4))
+    high, low = split(t_buf[...].reshape(256, 128))
+    u_buf[...] = mm(pick, high) + mm(pick, low)
+
+    @pl.loop(1, ROW)
+    def _(j):
+        pltpu.make_async_remote_copy(
+            src_ref=u_buf, dst_ref=v_buf.at[xc], send_sem=u_sem.at[0], recv_sem=u_sem.at[1],
+            device_id=in_row(j), device_id_type=MESH,
+        ).start()
+
+    v_buf[xc] = u_buf[...]
+    event(0, 1, 1)
     w_step(y)
-    event(0, 1, 1)
     event(0, 2, 0)
+    event(0, 2, 1)
+    w_arrived(RIGHT, 0, 1)
+    w_launch(RIGHT, 0, 1)
+    w_arrived(LEFT, 1, 1)
+    w_launch(LEFT, 1, 1)
     pltpu.make_async_copy(v_buf.at[seven], v_buf.at[seven], u_sem.at[1]).wait()
 
     @pl.loop(0, INT)
@@ -252,17 +261,12 @@
         a3[o, 192:, 128:256] = low
         a3[o, 192:, 256:384] = high
 
-    w_arrived(RIGHT, 0, 1)
-    w_launch(RIGHT, 0, 1)
-    w_arrived(LEFT, 1, 1)
-    w_launch(LEFT, 1, 1)
     process(0, 0)
     process(0, -1)
-    event(0, 2, 1)
     process(0, 1)
-    process(0, -2)
     event(0, 3, 0)
     begin(1)
+    process(0, -2)
     process(0, 2)
     event(0, 3, 1)
     process(0, -3)
@@ -316,32 +320,42 @@
 
         @pl.loop(0, COL)
         def _(q):
-            at = pl.ds(pl.multiple_of(q * 256, 256), 256)
+            to_row = lax.rem(y + q, COL)
+            at = pl.ds(pl.multiple_of(to_row * 256, 256), 256)
+            into = pl.ds(to_row * ROW, ROW)
             part = mm_nt(whi[half, at, :], both)
             part = part[:, :128] + (part[:, 128:] + mm_nt(wlo[half, at, :], high))
             part = part.reshape(ROW, 32, 128)
             if half == 0:
-                ct[a, :, q] = part
+                ct[a, into] = part
             else:
-                ct[a, :, q] += part
+                ct[a, into] += part
+
+                @pl.loop(0, ROW)
+                def _(n):
+                    to = to_row * ROW + lax.rem(xc + n, ROW)
+
+                    @pl.when(to != d)
+                    def _():
+                        pltpu.make_async_remote_copy(
+                            src_ref=ct.at[a, to], dst_ref=rs.at[a, d], send_sem=r_send.at[a], recv_sem=r_recv.at[a],
+                            device_id={"amp": to, "int": z}, device_id_type=MESH,
+                        ).start()
 
         if half == 1:
-            @pl.loop(1, ROW)
-            def _(j):
-                to = lax.rem(xc + j, ROW)
-                pltpu.make_async_remote_copy(
-                    src_ref=ct.at[a, to], dst_ref=rs.at[a, xc], send_sem=r_send.at[a], recv_sem=r_recv.at[a],
-                    device_id=in_row(j), device_id_type=MESH,
-                ).start()
-
-            rs[a, xc] = ct[a, xc]
+            rs[a, d] = ct[a, d]
+
+    others = pl.ds(0, PLANE - 1)
 
     def narrow(a):
-        pltpu.make_async_copy(ct.at[a, seven], rs.at[a, seven], r_recv.at[a]).wait()
-        total = rs[a, 0]
-        for n in range(1, ROW):
-            total += rs[a, n]
-        zs[:, 16 * a : 16 * a + 16, :] = total.reshape(128, 128).T.reshape(INT, 16, 128)
+        pltpu.make_async_copy(ct.at[a, others], rs.at[a, others], r_recv.at[a]).wait()
+        rows = []
+        for row in range(COL):
+            total = rs[a, row * ROW]
+            for n in range(1, ROW):
+                total += rs[a, row * ROW + n]
+            rows.append(total)
+        zs[:, 16 * a : 16 * a + 16, :] = jnp.concatenate(rows, axis=0).T.reshape(INT, 16, 128)
 
     def w_rest(way, halves):
         for h in halves:
@@ -349,24 +363,29 @@
 
     regroup(0, 0)
     regroup(0, 1)
+    w_rest(RIGHT, (1,))
+    w_step(lax.rem(y + 3, COL))
     event(1, 1, 0)
     lad_ref[:, 0:800] = acc0[:192, :]
-    event(1, 1, 1)
     store_0 = pltpu.make_async_copy(lad_ref.at[:, pl.ds(0, 768)], lad_hbm.at[:, pl.ds(0, 768)], out_sem.at[0])
     store_0.start()
+    event(1, 1, 1)
+    w_rest(LEFT, (0,))
+    w_step(lax.rem(y + 1, COL))
+    event(1, 2, 0)
     process(1, 0)
     process(1, -1)
-    event(1, 2, 0)
-    w_rest(RIGHT, (1,))
-    w_step(lax.rem(y + 3, COL))
     event(1, 2, 1)
+    w_arrived(RIGHT, 0, 2)
+    w_arrived(LEFT, 1, 2)
+    w_step(lax.rem(y + 2, COL))
+    event(1, 3, 0)
     begin(2)
-    w_rest(LEFT, (0,))
-    w_step(lax.rem(y + 1, COL))
-    event(1, 3, 0)
+    contract(0, 0)
+    event(1, 3, 1)
+    contract(0, 1)
     process(1, 1)
     process(1, -2)
-    event(1, 3, 1)
     process(1, 2)
     process(1, -3)
     process(1, 3)
@@ -374,16 +393,11 @@
     process(1, 4)
     regroup(1, 0)
     event(2, 1, 0)
-    w_arrived(RIGHT, 0, 2)
-    w_arrived(LEFT, 1, 2)
-    w_step(lax.rem(y + 2, COL))
     event(2, 1, 1)
-    contract(0, 0)
+    process(2, 0)
     event(2, 2, 0)
-    contract(0, 1)
+    process(2, -1)
     event(2, 2, 1)
-    process(2, 0)
-    process(2, -1)
     process(2, 1)
     event(2, 3, 0)
     contract(1, 0)
@@ -416,26 +430,15 @@
     total = zr[0]
     for n in range(1, INT):
         total += zr[n]
-    ys[...] = total
-
-    @pl.loop(1, COL)
-    def _(j):
-        pltpu.make_async_remote_copy(
-            src_ref=ys, dst_ref=yr.at[y], send_sem=y_sem.at[0], recv_sem=y_sem.at[1],
-            device_id=in_col(j), device_id_type=MESH,
-        ).start()
-
-    yr[y] = total
-    three = pl.ds(0, 3)
-    pltpu.make_async_copy(yr.at[three], yr.at[three], y_sem.at[1]).wait()
-    exact = dict(precision=lax.Precision.HIGHEST, preferred_element_type=F32)
-    nt = (((1,), (1,)), ((), ()))
-    r, c = iota((32, 128), 0), iota((32, 128), 1)
-    mine = jnp.where(c == 32 * y + r, 1.0, 0.0).astype(F32)
-    kept = lax.dot_general(mine, yr[...].reshape(128, 128), nt, **exact)
-    r, c = iota((128, 128), 0), iota((128, 128), 1)
-    order = (r == 32 * ((c >> 4) & 3) + 16 * (c & 1) + 8 * (c >> 6) + ((c >> 1) & 7))
-    kept = jnp.dot(kept, jnp.where(order, 1.0, 0.0).astype(F32), **exact)
+    total = total.T
+    m, r = iota((32, 128), 0), iota((32, 128), 1)
+    kept = jnp.zeros((32, 128), F32)
+    for row in range(COL):
+        match = ((m >> 3) & 1 == r >> 6) & (m >> 4 == r & 1) & (m & 7 == (r >> 1) & 7) & ((r >> 4) & 3 == row)
+        kept += jnp.dot(
+            total[32 * row : 32 * row + 32], jnp.where(match, 1.0, 0.0).astype(F32),
+            precision=lax.Precision.HIGHEST, preferred_element_type=F32,
+        )
     sum_ref[...] = jnp.where(mask[...] > 0.5, kept, jnp.zeros_like(kept))
 
     for copy in started:
@@ -447,9 +450,8 @@
             pltpu.make_async_copy(
                 msg.at[a, half, seven], rcv.at[a, half, seven], a_send.at[2 * a + half]
             ).wait()
-        pltpu.make_async_copy(ct.at[a, seven], rs.at[a, seven], r_send.at[a]).wait()
+        pltpu.make_async_copy(ct.at[a, others], rs.at[a, others], r_send.at[a]).wait()
     pltpu.make_async_copy(zs.at[seven], zr.at[seven], z_sem.at[0]).wait()
-    pltpu.make_async_copy(yr.at[three], yr.at[three], y_sem.at[0]).wait()
     store_0.wait()
     store_1.wait()
 
@@ -487,24 +489,21 @@
             pltpu.VMEM((2, 1024, 768), BF16),
             pltpu.VMEM((2, 2, ROW, 16, 768), F32),
             pltpu.VMEM((2, 2, ROW, 16, 768), F32),
-            pltpu.VMEM((2, ROW, COL, 32, 128), F32),
-            pltpu.VMEM((2, ROW, COL, 32, 128), F32),
+            pltpu.VMEM((2, PLANE, 32, 128), F32),
+            pltpu.VMEM((2, PLANE, 32, 128), F32),
             pltpu.VMEM((INT, 32, 128), F32),
             pltpu.VMEM((INT, 32, 128), F32),
             pltpu.VMEM((32, 128), F32),
-            pltpu.VMEM((COL, 32, 128), F32),
-            pltpu.VMEM((32, 128), F32),
             dma((3,)),
             dma((2,)),
-            dma((48,)),
-            dma((48,)),
+            dma((96,)),
+            dma((96,)),
             dma((2,)),
             dma((2,)),
             dma((6,)),
             dma((6,)),
             dma((4,)),
             dma((4,)),
-            dma((2,)),
             dma((2,)),
             dma((2,)),
             dma((2,)),

time: 117 us -> 107 us (0.915)
  Pallas kernels: 113 us -> 103 us
    pallas_call x1, Pallas kernels: 113 us -> 103 us  [per_device(): pl.pallas_call(body, out_shape=(jax.ShapeDtypeStruct((192, 1600), F32), j...]
where the time goes in v3:
time: 107 us
  Pallas kernels  103 us (96%)
  local copies, waits for them, and re-layouts  3.05 us (3%)
    pallas_call x1, Pallas kernels, per_device(): pl.pallas_call(body, out_shape=(jax.ShapeDtypeStruct((192, 1600), F32), j...  103 us
    unnamed x4, local copies, waits for them, and re-layouts  3.05 us

profile of v3, /device:TPU:1, one launch (start us, length us, event | category | flops | bytes accessed | tf_op | source)
XLA Modules:
  0.0 107.0 jit_solution(10701716355152288512)
XLA Ops:
  0.6 103.3 %shard_map.68 = (f32[192,1600]{1,0:T(8,128)}, f32[32,128]{1,0:T(8,128)}) custom-call(f32[192,1024]{1,0:T(8,128)} %amp_hbm.1, f32[1600,128]{1,0:T(8,128)} %bitcast.3, f32[12,25,1024]{2,1,0:T(8,128)} %w_hbm.1, s32[96]{0:T(128)} %occ_ref.1, s32[800]{0:T(1024)} %vir_ref.1), custom_call_target="tpu_custom_call" | custom-call | flops 8000000000 | bytes 8000000 | tf_op jit(solution)/shard_map/pallas_call | solution.py:464
  103.9 0.0 copy-start
  103.9 2.4 %copy.9 = f32[192,1600]{1,0:T(8,128)} copy(f32[192,1600]{1,0:T(8,128)} %get-tuple-element.8) | data formatting | bytes 2457600
  106.4 0.0 copy-done
  106.4 0.6 copy.10
Async XLA Ops:
  103.9 2.5 %copy-start = (f32[32,128]{1,0:T(8,128)S(1)}, f32[32,128]{1,0:T(8,128)}, u32[]{:S(2)}) copy-start(f32[32,128]{1,0:T(8,128)} %get-tuple-element.5) | copy-start | bytes 49156

commit v4 on v3

--- a/solution.py
+++ b/solution.py
@@ -70,13 +70,14 @@
 
     barrier = pltpu.get_barrier_semaphore()
 
-    @pl.loop(1, PLANE)
+    for j in (1, INT - 1, 2, INT - 2, 3, INT - 3, 4):
+        pl.semaphore_signal(barrier, inc=1, device_id=in_stack(j), device_id_type=MESH)
+    for j in (1, COL - 1):
+        pl.semaphore_signal(barrier, inc=1, device_id=in_col(j), device_id_type=MESH)
+
+    @pl.loop(1, ROW)
     def _(j):
-        pl.semaphore_signal(barrier, inc=1, device_id={"amp": lax.rem(d + j, PLANE), "int": z}, device_id_type=MESH)
-
-    @pl.loop(1, INT)
-    def _(j):
-        pl.semaphore_signal(barrier, inc=1, device_id=in_stack(j), device_id_type=MESH)
+        pl.semaphore_signal(barrier, inc=1, device_id=in_row(j), device_id_type=MESH)
 
     load_amp = pltpu.make_async_copy(amp_hbm, amp_ref, in_sem.at[0])
     load_slab = pltpu.make_async_copy(slab_hbm, slab.at[z], in_sem.at[1])
@@ -91,9 +92,10 @@
     def piece(way, c, j, q):
         hop = 1 if way == RIGHT else -1
         part = slab.at[around(-hop * (j - 1)), place(c, q), :]
+        source = slab_hbm.at[place(c, q), :] if j == 1 else part
         k = ((way * 3 + c) * 4 + (j - 1)) * 4 + q
         return pltpu.make_async_remote_copy(
-            src_ref=part, dst_ref=part, send_sem=ag_send.at[k], recv_sem=ag_recv.at[k],
+            src_ref=source, dst_ref=part, send_sem=ag_send.at[k], recv_sem=ag_recv.at[k],
             device_id={"amp": d, "int": around(hop)}, device_id_type=MESH,
         )
 
@@ -144,8 +146,7 @@
     pick = one_hot((c == 96 * ((r >> 4) & 1) + 12 * (r >> 5) + (r & 15)) & ((r & 15) < 12))
     high, low = split(amp_ref[:, here])
     s_buf[...] = (mm(pick, high) + mm(pick, low)).reshape(INT, 32, 128)
-    load_slab.wait()
-    pl.semaphore_wait(barrier, PLANE - 1 + INT - 1)
+    pl.semaphore_wait(barrier, INT - 1 + 2 + ROW - 1)
 
     @pl.loop(1, INT)
     def _(j):
@@ -192,28 +193,6 @@
     r, c = iota((400, 512), 0), iota((400, 512), 1)
     table[...] = one_hot((r == 200 * (c >> 8) + 25 * ((c >> 5) & 7) + (c & 31)) & ((c & 31) < 25))
 
-    sub, lane = iota((32, 128), 0), iota((32, 128), 1)
-    row_label = jnp.where(lane < 64, occ_ref[2 * z], occ_ref[2 * z + 1])
-    col_label = jnp.zeros((32, 128), jnp.int32) + occ_ref[d // 2]
-    first = 32 * lax.rem(d, 2)
-
-    def label_step(b, both):
-        rows, cols = both
-        rows = jnp.where((lane & 63) == b, rows ^ vir_ref[b], rows)
-        cols = jnp.where(sub + first == b, cols ^ vir_ref[b], cols)
-        return rows, cols
-
-    row_label, col_label = lax.fori_loop(0, 64, label_step, (row_label, col_label))
-    mask[...] = jnp.where(row_label == col_label, 1.0, 0.0).astype(F32)
-
-    for o in range(INT):
-        high, low = split(amp_ref[:, 128 * o : 128 * o + 128])
-        a3[o, :192, 0:128] = high
-        a3[o, :192, 128:256] = low
-        a3[o, :192, 256:384] = high
-
-    wpad[...] = jnp.zeros_like(wpad)
-
     def w_step(block):
         for k in range(12):
             wpad[32 * k : 32 * k + 25, :] = wg[block, 25 * k : 25 * k + 25, :]
@@ -245,8 +224,15 @@
 
     v_buf[xc] = u_buf[...]
     event(0, 1, 1)
+    for o in range(INT):
+        high, low = split(amp_ref[:, 128 * o : 128 * o + 128])
+        a3[o, :192, 0:128] = high
+        a3[o, :192, 128:256] = low
+        a3[o, :192, 256:384] = high
+
+    wpad[...] = jnp.zeros_like(wpad)
+    event(0, 2, 0)
     w_step(y)
-    event(0, 2, 0)
     event(0, 2, 1)
     w_arrived(RIGHT, 0, 1)
     w_launch(RIGHT, 0, 1)
@@ -260,7 +246,7 @@
         a3[o, 192:, 0:128] = high
         a3[o, 192:, 128:256] = low
         a3[o, 192:, 256:384] = high
-
+    load_slab.wait()
     process(0, 0)
     process(0, -1)
     process(0, 1)
@@ -271,8 +257,6 @@
     event(0, 3, 1)
     process(0, -3)
     process(0, 3)
-    last(0)
-    process(0, 4)
 
     def regroup(a, half):
         source = acc0[192:, 400 * half : 400 * half + 400] if a == 0 else accs[1 + half][192:, :]
@@ -361,47 +345,46 @@
         for h in halves:
             w_arrived(way, h, 1)
 
-    regroup(0, 0)
-    regroup(0, 1)
     w_rest(RIGHT, (1,))
     w_step(lax.rem(y + 3, COL))
+    last(0)
+    process(0, 4)
     event(1, 1, 0)
-    lad_ref[:, 0:800] = acc0[:192, :]
-    store_0 = pltpu.make_async_copy(lad_ref.at[:, pl.ds(0, 768)], lad_hbm.at[:, pl.ds(0, 768)], out_sem.at[0])
-    store_0.start()
+    regroup(0, 0)
     event(1, 1, 1)
+    regroup(0, 1)
+    event(1, 2, 0)
     w_rest(LEFT, (0,))
     w_step(lax.rem(y + 1, COL))
-    event(1, 2, 0)
+    event(1, 2, 1)
     process(1, 0)
     process(1, -1)
-    event(1, 2, 1)
+    process(1, 1)
+    event(1, 3, 0)
+    begin(2)
     w_arrived(RIGHT, 0, 2)
     w_arrived(LEFT, 1, 2)
     w_step(lax.rem(y + 2, COL))
-    event(1, 3, 0)
-    begin(2)
-    contract(0, 0)
     event(1, 3, 1)
-    contract(0, 1)
-    process(1, 1)
     process(1, -2)
     process(1, 2)
     process(1, -3)
     process(1, 3)
     last(1)
     process(1, 4)
+    event(2, 1, 0)
     regroup(1, 0)
-    event(2, 1, 0)
     event(2, 1, 1)
+    contract(0, 0)
+    event(2, 2, 0)
+    contract(0, 1)
+    event(2, 2, 1)
     process(2, 0)
-    event(2, 2, 0)
     process(2, -1)
-    event(2, 2, 1)
-    process(2, 1)
     event(2, 3, 0)
     contract(1, 0)
     event(2, 3, 1)
+    process(2, 1)
     process(2, -2)
     process(2, 2)
     process(2, -3)
@@ -409,11 +392,29 @@
     last(2)
     process(2, 4)
     regroup(1, 1)
+    lad_ref[:, 0:800] = acc0[:192, :]
+    store_0 = pltpu.make_async_copy(lad_ref.at[:, pl.ds(0, 768)], lad_hbm.at[:, pl.ds(0, 768)], out_sem.at[0])
+    store_0.start()
     lad_ref[:, 800:1200] = acc1[:192, :]
     lad_ref[:, 1200:1600] = acc2[:192, :]
     store_1 = pltpu.make_async_copy(lad_ref.at[:, pl.ds(768, 832)], lad_hbm.at[:, pl.ds(768, 832)], out_sem.at[1])
     store_1.start()
     narrow(0)
+
+    sub, lane = iota((32, 128), 0), iota((32, 128), 1)
+    row_label = jnp.where(lane < 64, occ_ref[2 * z], occ_ref[2 * z + 1])
+    col_label = jnp.zeros((32, 128), jnp.int32) + occ_ref[d // 2]
+    first = 32 * lax.rem(d, 2)
+
+    def label_step(b, both):
+        rows, cols = both
+        rows = jnp.where((lane & 63) == b, rows ^ vir_ref[b], rows)
+        cols = jnp.where(sub + first == b, cols ^ vir_ref[b], cols)
+        return rows, cols
+
+    row_label, col_label = lax.fori_loop(0, 64, label_step, (row_label, col_label))
+    mask[...] = jnp.where(row_label == col_label, 1.0, 0.0).astype(F32)
+
     contract(1, 1)
     narrow(1)
 
@@ -454,6 +455,22 @@
     pltpu.make_async_copy(zs.at[seven], zr.at[seven], z_sem.at[0]).wait()
     store_0.wait()
     store_1.wait()
+
+
+def hand_on(lad_in, sum_in, lad_out, sum_out, held, held_sum, sem):
+    moves = [(sum_in, held_sum, sum_out, 8)]
+    for n in range(8):
+        rows = pl.ds(24 * n, 24)
+        moves.append((lad_in.at[rows, :], held.at[rows, :], lad_out.at[rows, :], n))
+    loads = [pltpu.make_async_copy(a, b, sem.at[n]) for a, b, _, n in moves]
+    stores = [pltpu.make_async_copy(b, c, sem.at[9 + n]) for _, b, c, n in moves]
+    for copy in loads:
+        copy.start()
+    for load, store in zip(loads, stores):
+        load.wait()
+        store.start()
+    for copy in stores:
+        copy.wait()
 
 
 def per_device(amplitudes, slab_integrals, cycle_integrals, occ_irrep, vir_irrep):
@@ -513,6 +530,16 @@
         ),
         cost_estimate=pl.CostEstimate(flops=8_000_000_000, bytes_accessed=8_000_000, transcendentals=0),
     )(amplitudes, slab_integrals.T, cycle_integrals, occ_irrep, vir_irrep)
+    ladder, sums = pl.pallas_call(
+        hand_on,
+        out_shape=(
+            jax.ShapeDtypeStruct((192, 1600), F32),
+            jax.ShapeDtypeStruct((32, 128), F32),
+        ),
+        in_specs=[anywhere] * 2,
+        out_specs=(anywhere, anywhere),
+        scratch_shapes=[pltpu.VMEM((192, 1600), F32), pltpu.VMEM((32, 128), F32), dma((18,))],
+    )(ladder, sums)
     return ladder, sums.T
 
 

time: 107 us -> 105 us (0.981)
  local copies, waits for them, and re-layouts: 3.05 us -> 0 us
    unnamed x4 -> x0, local copies, waits for them, and re-layouts: 3.05 us -> none
    pallas_call x0 -> x1, Pallas kernels: none -> 2.22 us  [per_device(): pl.pallas_call(hand_on, out_shape=(jax.ShapeDtypeStruct((192, 1600), F32)...]
    pallas_call x1, Pallas kernels: 103 us -> 102 us  [per_device(): pl.pallas_call(body, out_shape=(jax.ShapeDtypeStruct((192, 1600), F32), j...]
where the time goes in v4:
time: 105 us
  Pallas kernels  104 us (99%)
    pallas_call x1, Pallas kernels, per_device(): pl.pallas_call(body, out_shape=(jax.ShapeDtypeStruct((192, 1600), F32), j...  102 us
    pallas_call x1, Pallas kernels, per_device(): pl.pallas_call(hand_on, out_shape=(jax.ShapeDtypeStruct((192, 1600), F32)...  2.22 us

profile of v4, /device:TPU:1, one launch (start us, length us, event | category | flops | bytes accessed | tf_op | source)
XLA Modules:
  0.0 104.6 jit_solution(9556924844756559598)
XLA Ops:
  0.6 101.7 %shard_map.68 = (f32[192,1600]{1,0:T(8,128)}, f32[32,128]{1,0:T(8,128)}) custom-call(f32[192,1024]{1,0:T(8,128)} %amp_hbm.1, f32[1600,128]{1,0:T(8,128)} %bitcast.2, f32[12,25,1024]{2,1,0:T(8,128)} %w_hbm.1, s32[96]{0:T(128)} %occ_ref.1, s32[800]{0:T(1024)} %vir_ref.1), custom_call_target="tpu_custom_call" | custom-call | flops 8000000000 | bytes 8000000 | tf_op jit(solution)/shard_map/pallas_call | solution.py:481
  102.3 2.2 %shard_map.69 = (f32[192,1600]{1,0:T(8,128)}, f32[32,128]{1,0:T(8,128)}) custom-call(f32[192,1600]{1,0:T(8,128)} %get-tuple-element.6.lad_in, f32[32,128]{1,0:T(8,128)} %get-tuple-element.7.sum_in), custom_call_target="tpu_custom_call" | custom-call | tf_op jit(solution)/shard_map/pallas_call | solution.py:533

commit v5 on v4

--- a/solution.py
+++ b/solution.py
@@ -12,7 +12,7 @@
 INT = 8
 ROW = 8
 COL = 4
-PLANE = ROW * COL
+CHIPS = 16
 WIDTHS = (800, 400, 400)
 STARTS = (0, 800, 1200)
 PIECES = tuple(
@@ -47,13 +47,15 @@
     amp_hbm, slab_hbm, w_hbm, occ_ref, vir_ref,
     lad_hbm, sum_ref,
     amp_ref, w_ref, lad_ref, slab, a3, acc0, acc1, acc2, table, s_buf, t_buf, u_buf, v_buf,
-    wg, wpad, whi, wlo, msg, rcv, ct, rs, zs, zr, mask,
-    in_sem, out_sem, ag_send, ag_recv, s_sem, u_sem, w_send, w_recv, a_send, a_recv, r_send, r_recv, z_sem,
+    wg, wpad, whi, wlo, msg, rcv, ct, cs, rs, zs, zr, mask,
+    in_sem, out_sem, ag_send, ag_recv, s_sem, u_sem, w_send, w_recv, a_send, a_recv, c_send, c_recv, r_send, r_recv, z_sem,
 ):
     d = lax.axis_index("amp")
     z = lax.axis_index("int")
     y = d // ROW
     xc = lax.rem(d, ROW)
+    core = lax.rem(d, 2)
+    chip = d // 2
     accs = (acc0, acc1, acc2)
 
     def around(step):
@@ -306,38 +308,45 @@
         def _(q):
             to_row = lax.rem(y + q, COL)
             at = pl.ds(pl.multiple_of(to_row * 256, 256), 256)
-            into = pl.ds(to_row * ROW, ROW)
             part = mm_nt(whi[half, at, :], both)
             part = part[:, :128] + (part[:, 128:] + mm_nt(wlo[half, at, :], high))
-            part = part.reshape(ROW, 32, 128)
-            if half == 0:
-                ct[a, into] = part
-            else:
-                ct[a, into] += part
-
-                @pl.loop(0, ROW)
-                def _(n):
-                    to = to_row * ROW + lax.rem(xc + n, ROW)
-
-                    @pl.when(to != d)
-                    def _():
-                        pltpu.make_async_remote_copy(
-                            src_ref=ct.at[a, to], dst_ref=rs.at[a, d], send_sem=r_send.at[a], recv_sem=r_recv.at[a],
-                            device_id={"amp": to, "int": z}, device_id_type=MESH,
-                        ).start()
+            part = part.reshape(COL, 2, 32, 128)
+            into = pl.ds(to_row * COL, COL)
+            for n in range(2):
+                if half == 0:
+                    ct[a, n, into] = part[:, n]
+                else:
+                    ct[a, n, into] += part[:, n]
 
         if half == 1:
-            rs[a, d] = ct[a, d]
-
-    others = pl.ds(0, PLANE - 1)
+            pltpu.make_async_remote_copy(
+                src_ref=ct.at[a, 1 - core], dst_ref=cs.at[a], send_sem=c_send.at[a], recv_sem=c_recv.at[a],
+                device_id={"amp": d + 1 - 2 * core, "int": z}, device_id_type=MESH,
+            ).start()
+
+    others = pl.ds(0, CHIPS - 1)
+
+    def spread(a):
+        pltpu.make_async_copy(cs.at[a], cs.at[a], c_recv.at[a]).wait()
+
+        @pl.loop(1, CHIPS)
+        def _(n):
+            to = lax.rem(chip + n, CHIPS)
+            ct[a, core, to] += cs[a, to]
+            pltpu.make_async_remote_copy(
+                src_ref=ct.at[a, core, to], dst_ref=rs.at[a, chip], send_sem=r_send.at[a], recv_sem=r_recv.at[a],
+                device_id={"amp": to * 2 + core, "int": z}, device_id_type=MESH,
+            ).start()
+
+        rs[a, chip] = ct[a, core, chip] + cs[a, chip]
 
     def narrow(a):
-        pltpu.make_async_copy(ct.at[a, others], rs.at[a, others], r_recv.at[a]).wait()
+        pltpu.make_async_copy(rs.at[a, others], rs.at[a, others], r_recv.at[a]).wait()
         rows = []
         for row in range(COL):
-            total = rs[a, row * ROW]
-            for n in range(1, ROW):
-                total += rs[a, row * ROW + n]
+            total = rs[a, row * COL]
+            for n in range(1, COL):
+                total += rs[a, row * COL + n]
             rows.append(total)
         zs[:, 16 * a : 16 * a + 16, :] = jnp.concatenate(rows, axis=0).T.reshape(INT, 16, 128)
 
@@ -382,6 +391,7 @@
     process(2, 0)
     process(2, -1)
     event(2, 3, 0)
+    spread(0)
     contract(1, 0)
     event(2, 3, 1)
     process(2, 1)
@@ -416,6 +426,7 @@
     mask[...] = jnp.where(row_label == col_label, 1.0, 0.0).astype(F32)
 
     contract(1, 1)
+    spread(1)
     narrow(1)
 
     @pl.loop(1, INT)
@@ -451,7 +462,8 @@
             pltpu.make_async_copy(
                 msg.at[a, half, seven], rcv.at[a, half, seven], a_send.at[2 * a + half]
             ).wait()
-        pltpu.make_async_copy(ct.at[a, others], rs.at[a, others], r_send.at[a]).wait()
+        pltpu.make_async_copy(cs.at[a], cs.at[a], c_send.at[a]).wait()
+        pltpu.make_async_copy(rs.at[a, others], rs.at[a, others], r_send.at[a]).wait()
     pltpu.make_async_copy(zs.at[seven], zr.at[seven], z_sem.at[0]).wait()
     store_0.wait()
     store_1.wait()
@@ -506,8 +518,9 @@
             pltpu.VMEM((2, 1024, 768), BF16),
             pltpu.VMEM((2, 2, ROW, 16, 768), F32),
             pltpu.VMEM((2, 2, ROW, 16, 768), F32),
-            pltpu.VMEM((2, PLANE, 32, 128), F32),
-            pltpu.VMEM((2, PLANE, 32, 128), F32),
+            pltpu.VMEM((2, 2, CHIPS, 32, 128), F32),
+            pltpu.VMEM((2, CHIPS, 32, 128), F32),
+            pltpu.VMEM((2, CHIPS, 32, 128), F32),
             pltpu.VMEM((INT, 32, 128), F32),
             pltpu.VMEM((INT, 32, 128), F32),
             pltpu.VMEM((32, 128), F32),
@@ -521,6 +534,8 @@
             dma((6,)),
             dma((4,)),
             dma((4,)),
+            dma((2,)),
+            dma((2,)),
             dma((2,)),
             dma((2,)),
             dma((2,)),

time: 105 us -> 104 us (level); the launches traced: 105 us -> 102 us
  Pallas kernels: 104 us -> 102 us
    pallas_call x1, Pallas kernels: 102 us -> 99.6 us  [per_device(): pl.pallas_call(body, out_shape=(jax.ShapeDtypeStruct((192, 1600), F32), j...]
where the time goes in v5:
time: 104 us; the launch traced here: 102 us
  Pallas kernels  102 us (98%)
    pallas_call x1, Pallas kernels, per_device(): pl.pallas_call(body, out_shape=(jax.ShapeDtypeStruct((192, 1600), F32), j...  99.6 us
    pallas_call x1, Pallas kernels, per_device(): pl.pallas_call(hand_on, out_shape=(jax.ShapeDtypeStruct((192, 1600), F32)...  2.22 us

profile of v5, /device:TPU:1, one launch (start us, length us, event | category | flops | bytes accessed | tf_op | source)
XLA Modules:
  0.0 102.5 jit_solution(7741711312508014585)
XLA Ops:
  0.6 99.6 %shard_map.68 = (f32[192,1600]{1,0:T(8,128)}, f32[32,128]{1,0:T(8,128)}) custom-call(f32[192,1024]{1,0:T(8,128)} %amp_hbm.1, f32[1600,128]{1,0:T(8,128)} %bitcast.2, f32[12,25,1024]{2,1,0:T(8,128)} %w_hbm.1, s32[96]{0:T(128)} %occ_ref.1, s32[800]{0:T(1024)} %vir_ref.1), custom_call_target="tpu_custom_call" | custom-call | flops 8000000000 | bytes 8000000 | tf_op jit(solution)/shard_map/pallas_call | solution.py:493
  100.3 2.2 %shard_map.69 = (f32[192,1600]{1,0:T(8,128)}, f32[32,128]{1,0:T(8,128)}) custom-call(f32[192,1600]{1,0:T(8,128)} %get-tuple-element.6.lad_in, f32[32,128]{1,0:T(8,128)} %get-tuple-element.7.sum_in), custom_call_target="tpu_custom_call" | custom-call | tf_op jit(solution)/shard_map/pallas_call | solution.py:548
